TPU v7x, 512 devices: a whole 4x4x16 slice. The times are simulated.
512 devices in a mesh: cp: 64 (over x, y, z_hi), hd: 8 (over z_lo, core).
Axes of the slice: x: 4, y: 4, z: 16 (z_hi: 4, z_lo: 4; z = z_hi * 4 + z_lo), core: 2. Of those that a mesh axis runs over, the one named last changes fastest.
Arguments:
- queries: bfloat16 [32768, 8192], P(('cp', 'hd')), may hold values from -8 to 8
- key_vectors: bfloat16 [32768, 1024], P(('cp', 'hd')), may hold values from -8 to 8
- value_vectors: bfloat16 [32768, 1024], P(('cp', 'hd')), may hold values from -6 to 6
- out_grad: bfloat16 [32768, 8192], P(('cp', 'hd')), may hold values from -6 to 6
- doc_lengths: int32 [128], replicated, may hold values from 1 to 512, 32768 in all
Outputs:
- attended: bfloat16 [32768, 8192], P(('cp', 'hd'))
- query_grad: bfloat16 [32768, 8192], P(('cp', 'hd'))
- key_grad: bfloat16 [32768, 1024], P(('cp', 'hd'))
- value_grad: bfloat16 [32768, 1024], P(('cp', 'hd'))
Inputs may be any that keep to these rules, and one draw needn't show every extreme that they name: `doc_lengths`: the lengths sum to 32768; the longest document has exactly 512 tokens.
All inputs are finite; a program needn't handle non-finite values.
Results may differ from a plain program's by a relative error of at most 0.027.
Values may be sent and summed in bfloat16 or wider, within the bound.
A program may use at most 128 MiB of HBM per device.

v0:
```python
import jax
import jax.numpy as jnp
from jax import lax
from jax.sharding import PartitionSpec as P

DH = 128


NEGATIVE = -1e30


def from_behind(block, axis, distance):
    devices = range(lax.axis_size(axis))
    route = [(i - distance, i) for i in devices if i - distance in devices]
    return lax.ppermute(block, axis, route)


def segment_of(positions, doc_lengths):
    doc_ends = jnp.cumsum(doc_lengths)
    return jnp.sum((doc_ends[None, :] <= positions[:, None]).astype(jnp.int32), axis=1)


def per_device(queries, key_vectors, value_vectors, out_grad, doc_lengths):
    query_local, key_local, value_local, grad_local = (
        lax.all_to_all(queries, "hd", split_axis=1, concat_axis=0, tiled=True),
        lax.all_to_all(key_vectors, "hd", split_axis=1, concat_axis=0, tiled=True),
        lax.all_to_all(value_vectors, "hd", split_axis=1, concat_axis=0, tiled=True),
        lax.all_to_all(out_grad, "hd", split_axis=1, concat_axis=0, tiled=True),
    )
    row_count = query_local.shape[0]
    kv_heads = key_local.shape[1] // DH
    group_size = query_local.shape[1] // (kv_heads * DH)
    score_scale = DH ** (-0.5)
    query_heads = query_local.reshape(row_count, kv_heads, group_size, DH)
    grad_heads = grad_local.reshape(row_count, kv_heads, group_size, DH)
    cp_index = lax.axis_index("cp")
    row_ids = jnp.arange(row_count, dtype=jnp.int32)
    query_pos = cp_index * row_count + row_ids
    query_seg = segment_of(query_pos, doc_lengths)

    def allowed_for(distance):
        key_pos = (cp_index - distance) * row_count + row_ids
        key_seg = segment_of(key_pos, doc_lengths)
        allowed = (
            (key_pos[None, :] >= 0)
            & (key_pos[None, :] <= query_pos[:, None])
            & (key_seg[None, :] == query_seg[:, None])
        )
        return allowed[:, None, None, :]

    def scores_for(key_block):
        key_heads = key_block.reshape(row_count, kv_heads, DH)
        return (
            jnp.einsum("thgd,shd->thgs", query_heads, key_heads, preferred_element_type=jnp.float32)
            * score_scale
        )

    def forward_step(carried, kv_pair, distance):
        allowed = allowed_for(distance)
        run_max, run_sum, run_out = carried
        scores = scores_for(kv_pair[0])
        value_heads = kv_pair[1].reshape(row_count, kv_heads, DH)
        block_max = jnp.max(jnp.where(allowed, scores, NEGATIVE), axis=-1)
        weights = jnp.where(allowed, jnp.exp(scores - block_max[..., None]), 0.0)
        block_sum = jnp.sum(weights, axis=-1)
        partial_value = jnp.einsum(
            "thgs,shd->thgd",
            weights.astype(jnp.bfloat16),
            value_heads,
            preferred_element_type=jnp.float32,
        )
        new_max = jnp.maximum(run_max, block_max)
        old_factor = jnp.exp(run_max - new_max)
        new_factor = jnp.exp(block_max - new_max)
        return (
            new_max,
            run_sum * old_factor + block_sum * new_factor,
            run_out * old_factor[..., None] + partial_value * new_factor[..., None],
        )

    start_max = jnp.full((row_count, kv_heads, group_size), NEGATIVE, jnp.float32)
    start_sum = jnp.zeros((row_count, kv_heads, group_size), jnp.float32)
    start_out = jnp.zeros((row_count, kv_heads, group_size, DH), jnp.float32)
    carried = forward_step((start_max, start_sum, start_out), (key_local, value_local), 0)
    stored = []
    visiting = (key_local, value_local)
    distance = 1
    visiting = from_behind((visiting[0], visiting[1]), "cp", 1)
    stored.append(visiting)
    carried = forward_step(carried, visiting, distance)
    run_max, run_sum, run_out = carried
    out_heads = (run_out / run_sum[..., None]).astype(jnp.bfloat16)
    log_norm = run_max + jnp.log(run_sum)
    attended = lax.all_to_all(
        out_heads.reshape(row_count, kv_heads * group_size * DH),
        "hd",
        split_axis=0,
        concat_axis=1,
        tiled=True,
    )
    out_dot = jnp.sum(grad_heads.astype(jnp.float32) * out_heads.astype(jnp.float32), axis=-1)

    def grads_for(kv_pair, allowed):
        key_heads = kv_pair[0].reshape(row_count, kv_heads, DH)
        value_heads = kv_pair[1].reshape(row_count, kv_heads, DH)
        scores = scores_for(kv_pair[0])
        probabilities = jnp.where(allowed, jnp.exp(scores - log_norm[..., None]), 0.0)
        prob_grad = jnp.einsum(
            "thgd,shd->thgs", grad_heads, value_heads, preferred_element_type=jnp.float32
        )
        score_grad = (probabilities * (prob_grad - out_dot[..., None])).astype(jnp.bfloat16)
        rounded_probs = probabilities.astype(jnp.bfloat16)
        query_part = (
            jnp.einsum("thgs,shd->thgd", score_grad, key_heads, preferred_element_type=jnp.float32)
            * score_scale
        )
        key_part = (
            jnp.einsum(
                "thgs,thgd->shd", score_grad, query_heads, preferred_element_type=jnp.float32
            )
            * score_scale
        )
        value_part = jnp.einsum(
            "thgs,thgd->shd", rounded_probs, grad_heads, preferred_element_type=jnp.float32
        )
        return (
            query_part,
            key_part.reshape(row_count, kv_heads * DH),
            value_part.reshape(row_count, kv_heads * DH),
        )

    def backward_step(kv_pair, distance):
        allowed = allowed_for(distance)
        return grads_for(kv_pair, allowed)

    query_sum, key_own, value_own = backward_step((key_local, value_local), 0)
    moving = (key_local, value_local)
    distance = 1
    moving = from_behind((moving[0], moving[1]), "cp", 1)
    query_part, key_part, value_part = backward_step(moving, distance)
    query_sum = query_sum + query_part
    homeward = (
        from_behind(key_part.astype(jnp.bfloat16), "cp", -distance).astype(key_part.dtype),
        from_behind(value_part.astype(jnp.bfloat16), "cp", -distance).astype(value_part.dtype),
    )
    key_back = homeward[0]
    value_back = homeward[1]
    returned = (key_back, value_back)
    query_local_grad = query_sum.astype(jnp.bfloat16).reshape(row_count, kv_heads * group_size * DH)
    key_local_grad = (key_own + returned[0]).astype(jnp.bfloat16)
    value_local_grad = (value_own + returned[1]).astype(jnp.bfloat16)
    query_grad, key_grad, value_grad = (
        lax.all_to_all(query_local_grad, "hd", split_axis=0, concat_axis=1, tiled=True),
        lax.all_to_all(key_local_grad, "hd", split_axis=0, concat_axis=1, tiled=True),
        lax.all_to_all(value_local_grad, "hd", split_axis=0, concat_axis=1, tiled=True),
    )
    return (attended, query_grad, key_grad, value_grad)


def solution(mesh):
    return jax.shard_map(
        per_device,
        mesh=mesh,
        in_specs=(
            P(("cp", "hd"), None),
            P(("cp", "hd"), None),
            P(("cp", "hd"), None),
            P(("cp", "hd"), None),
            P(),
        ),
        out_specs=(
            P(("cp", "hd"), None),
            P(("cp", "hd"), None),
            P(("cp", "hd"), None),
            P(("cp", "hd"), None),
        ),
        check_vma=False,
    )
```

profile of v0, /device:TPU:6, one launch (start us, length us, event | category | flops | bytes accessed | tf_op | source)
XLA Modules:
  0.0 248.8 jit_solution(18084782565873629322)
XLA Ops:
  0.6 0.0 copy-start
  0.6 0.9 copy-done
  1.5 0.7 copy_bitcast_fusion.5
  2.2 5.9 %all-to-all-start = ((bf16[64,8,128]{2,0,1:T(8,128)(2,1)}), bf16[64,8,128]{2,0,1:T(8,128)(2,1)}, u32[]{:S(2)}, u32[]{:S(2)}) async-start(bf16[64,8,128]{2,0,1:T(8,128)(2,1)} %copy_bitcast_fusion.5), calls=%async_computation | async-start | bytes 262144 | tf_op jit(solution)/shard_map/all_to_all | solution.py:26
  8.1 1.6 copy_bitcast_fusion.4
  9.7 5.3 %all-to-all-done = bf16[64,8,128]{2,0,1:T(8,128)(2,1)} async-done(((bf16[64,8,128]{2,0,1:T(8,128)(2,1)}), bf16[64,8,128]{2,0,1:T(8,128)(2,1)}, u32[]{:S(2)}, u32[]{:S(2)}) %all-to-all-start) | async-done | bytes 131104 | tf_op jit(solution)/shard_map/all_to_all | solution.py:26
  15.0 3.4 %all-to-all-start.2 = ((bf16[64,8,128]{2,0,1:T(8,128)(2,1)}), bf16[64,8,128]{2,0,1:T(8,128)(2,1)S(1)}, u32[]{:S(2)}, u32[]{:S(2)}) async-start(bf16[64,8,128]{2,0,1:T(8,128)(2,1)} %copy_bitcast_fusion.4), calls=%async_computation.2 | async-start | bytes 262144 | tf_op jit(solution)/shard_map/all_to_all | solution.py:27
  18.4 2.3 copy.177
  20.7 4.4 %all-to-all-done.2 = bf16[64,8,128]{2,0,1:T(8,128)(2,1)S(1)} async-done(((bf16[64,8,128]{2,0,1:T(8,128)(2,1)}), bf16[64,8,128]{2,0,1:T(8,128)(2,1)S(1)}, u32[]{:S(2)}, u32[]{:S(2)}) %all-to-all-start.2) | async-done | bytes 131104 | tf_op jit(solution)/shard_map/all_to_all | solution.py:27
  25.1 3.6 %all-to-all-start.1 = ((bf16[64,8,1024]{2,0,1:T(8,128)(2,1)}), bf16[64,8,1024]{2,0,1:T(8,128)(2,1)S(1)}, u32[]{:S(2)}, u32[]{:S(2)}) async-start(bf16[64,8,1024]{2,0,1:T(8,128)(2,1)} %bitcast.278), calls=%async_computation.1 | async-start | bytes 2097152 | tf_op jit(solution)/shard_map/all_to_all | solution.py:25
  28.7 2.3 copy.176
  31.0 24.2 %all-to-all-done.1 = bf16[64,8,1024]{2,0,1:T(8,128)(2,1)S(1)} async-done(((bf16[64,8,1024]{2,0,1:T(8,128)(2,1)}), bf16[64,8,1024]{2,0,1:T(8,128)(2,1)S(1)}, u32[]{:S(2)}, u32[]{:S(2)}) %all-to-all-start.1) | async-done | bytes 1048608 | tf_op jit(solution)/shard_map/all_to_all | solution.py:25
  55.2 3.6 %all-to-all-start.4 = ((bf16[64,8,1024]{2,0,1:T(8,128)(2,1)}), bf16[64,8,1024]{2,0,1:T(8,128)(2,1)S(1)}, u32[]{:S(2)}, u32[]{:S(2)}) async-start(bf16[64,8,1024]{2,0,1:T(8,128)(2,1)} %bitcast.277), calls=%async_computation.4 | async-start | bytes 2097152 | tf_op jit(solution)/shard_map/all_to_all | solution.py:28
  58.8 0.1 copy.100
  58.9 0.2 reduce-window.8
  59.1 0.1 reduce.5
  59.2 0.4 convert_reduce_fusion
  59.6 9.1 %collective-permute-start = (bf16[512,128]{1,0:T(8,128)(2,1)}, bf16[512,128]{1,0:T(8,128)(2,1)}, u32[]{:S(2)}, u32[]{:S(2)}) collective-permute-start(bf16[512,128]{1,0:T(8,128)(2,1)} %bitcast.2), channel_id=1, source_target_pairs={{0,8},{8,16},{16,24},{24,32},{32,40},{40,48},{48,56},{56,64},{64,7... | collective-permute-start | bytes 393224 | tf_op jit(solution)/shard_map/ppermute | solution.py:15
  68.7 1.4 compare_and_fusion.1
  70.1 0.8 copy.108
  70.9 7.1 %collective-permute-start.1 = (bf16[512,128]{0,1:T(8,128)(2,1)}, bf16[512,128]{0,1:T(8,128)(2,1)}, u32[]{:S(2)}, u32[]{:S(2)}) collective-permute-start(bf16[512,128]{0,1:T(8,128)(2,1)} %copy.108), channel_id=1, source_target_pairs={{0,8},{8,16},{16,24},{24,32},{32,40},{40,48},{48,56},{56,64},{64,7... | collective-permute-start | bytes 393224 | tf_op jit(solution)/shard_map/ppermute | solution.py:15
  78.0 0.3 copy.143
  78.3 7.0 %all-to-all-done.4 = bf16[64,8,1024]{2,0,1:T(8,128)(2,1)S(1)} async-done(((bf16[64,8,1024]{2,0,1:T(8,128)(2,1)}), bf16[64,8,1024]{2,0,1:T(8,128)(2,1)S(1)}, u32[]{:S(2)}, u32[]{:S(2)}) %all-to-all-start.4) | async-done | bytes 1048608 | tf_op jit(solution)/shard_map/all_to_all | solution.py:28
  85.3 0.3 copy.144
  85.5 0.0 copy-start.6
  85.6 17.6 %collective-permute-done = bf16[512,128]{1,0:T(8,128)(2,1)} collective-permute-done((bf16[512,128]{1,0:T(8,128)(2,1)}, bf16[512,128]{1,0:T(8,128)(2,1)}, u32[]{:S(2)}, u32[]{:S(2)}) %collective-permute-start) | collective-permute-done | bytes 131104 | tf_op jit(solution)/shard_map/ppermute | solution.py:15
  103.1 2.6 %fusion.2 = (f32[512,8]{0,1:T(8,128)S(1)}, f32[512,512,8]{1,0,2:T(8,128)S(1)}) fusion(pred[512,512]{0,1:T(8,128)(4,1)} %get-tuple-element.13, bf16[512,8,128]{2,1,0:T(8,128)(2,1)S(1)} %bitcast.279, bf16[512,128]{1,0:T(8,128)(2,1)} %collective-permute-done), kind=kOutput, calls=%fused_computation.9 | convolution fusion | flops 543158272 | bytes 9846784 | tf_op jit(solution)/shard_map/thgd,shd->thgs/dot_general | solution.py:54
  105.8 1.7 fusion.16
  107.5 2.6 %fusion.7 = (f32[512,8]{0,1:T(8,128)S(1)}, f32[512,512,8]{1,0,2:T(8,128)S(1)}) fusion(pred[512,512]{0,1:T(8,128)(4,1)S(1)} %get-tuple-element.12, bf16[512,128,1]{1,0,2:T(8,128)(2,1)} %bitcast.3, bf16[512,8,128]{2,1,0:T(8,128)(2,1)S(1)} %bitcast.280), kind=kOutput, calls=%fused_computation.17 | convolution fusion | flops 543158272 | bytes 9846784 | tf_op jit(solution)/shard_map/thgd,shd->thgs/dot_general | solution.py:54
  110.2 1.7 fusion.13
  111.9 0.0 copy-start.9
  111.9 0.6 log_add_fusion
  112.6 2.3 fusion.55
  114.9 5.5 %collective-permute-start.3 = (bf16[512,128]{1,0:T(8,128)(2,1)}, bf16[512,128]{1,0:T(8,128)(2,1)}, u32[]{:S(2)}, u32[]{:S(2)}) collective-permute-start(bf16[512,128]{1,0:T(8,128)(2,1)} %fusion.55), channel_id=1, source_target_pairs={{8,0},{16,8},{24,16},{32,24},{40,32},{48,40},{56,48},{64,56},{72,6... | collective-permute-start | bytes 393224 | tf_op jit(solution)/shard_map/ppermute | solution.py:15
  120.5 3.1 %fusion.24 = f32[512,8,128]{0,2,1:T(8,128)} fusion(bf16[512,128,1]{1,0,2:T(8,128)(2,1)S(1)} %bitcast.298, f32[512,512,8]{1,0,2:T(8,128)S(1)} %get-tuple-element.17, f32[512,8]{0,1:T(8,128)S(1)} %get-tuple-element.16, pred[512,512]{0,1:T(8,128)(4,1)S(1)} %get-tuple-element.12), kind=kOutput, calls=%fused_computation.34 | convolution fusion | flops 545259520 | bytes 10895360 | tf_op jit(solution)/shard_map/thgs,shd->thgd/dot_general | solution.py:66
  123.6 0.2 bitcast_convert_fusion
  123.8 0.5 copy.145
  124.3 1.9 copy.114
  126.2 8.1 %multiply_reduce_fusion = (f32[512,8]{0,1:T(8,128)S(1)}, bf16[512,1,8,128]{0,3,2,1:T(8,128)(2,1)}) fusion(f32[512,1,8,128]{0,3,2,1:T(8,128)} %copy.114, f32[512,8]{0,1:T(8,128)} %get-tuple-element.7, f32[512,8]{0,1:T(8,128)} %get-tuple-element.8, f32[512,512,8]{1,0,2:T(8,128)} %copy-done.2, f32[512,8]{0,1:T(8,128)S(1)} %get-tuple-element.14, ...), kind=kOutput, calls=%fused_computation.50 | convolution fusion | flops 550498304 | bytes 14139392 | tf_op jit(solution)/shard_map/thgs,shd->thgd/dot_general | solution.py:66
  134.4 5.1 %fusion.23 = bf16[512,8,512]{0,2,1:T(8,128)(2,1)S(1)} fusion(f32[512,512,8]{1,0,2:T(8,128)} %copy-done.2, f32[512,8]{0,1:T(8,128)S(1)} %get-tuple-element.18, f32[512,8]{0,1:T(8,128)S(1)} %copy-done.12, pred[512,512]{0,1:T(8,128)(4,1)S(1)} %copy-done.5, bf16[512,8,128]{2,1,0:T(8,128)(2,1)S(1)} %bitcast.292, bf16[512,128]{0,1:T(8,128)(2,1)} %collective-permute-done.1), kind=kOutput, calls=%fused_computation.33 | convolution fusion | flops 549453824 | bytes 14057472 | tf_op jit(solution)/shard_map/thgd,shd->thgs/dot_general | solution.py:108
  139.6 2.0 copy-done.3
  141.5 1.2 fusion.58
  142.8 0.0 copy-start.10
  142.8 2.8 %collective-permute-start.2 = (bf16[512,128]{1,0:T(8,128)(2,1)S(1)}, bf16[512,128]{1,0:T(8,128)(2,1)S(1)}, u32[]{:S(2)}, u32[]{:S(2)}) collective-permute-start(bf16[512,128]{1,0:T(8,128)(2,1)S(1)} %fusion.58), channel_id=1, source_target_pairs={{8,0},{16,8},{24,16},{32,24},{40,32},{48,40},{56,48},{64,56},{72,6... | collective-permute-start | bytes 393224 | tf_op jit(solution)/shard_map/ppermute | solution.py:15
  145.6 5.8 %add_convert_fusion = bf16[512,128]{1,0:T(8,128)(2,1)} fusion(bf16[512,128]{1,0:T(8,128)(2,1)} %collective-permute-done.3, bf16[512,8,128]{2,1,0:T(8,128)(2,1)S(1)} %bitcast.293, f32[512,512,8]{1,0,2:T(8,128)} %copy-done.1, f32[512,8]{0,1:T(8,128)S(1)} %copy-done.12, pred[512,512]{0,1:T(8,128)(4,1)S(1)} %get-tuple-element.12), kind=kOutput, calls=%fused_computation.76 | convolution fusion | flops 545456128 | bytes 9977856 | tf_op jit(solution)/shard_map/thgs,thgd->shd/dot_general | solution.py:123
  151.4 13.8 %all-to-all-start.7 = ((bf16[8,64,128]{2,1,0:T(8,128)(2,1)}), bf16[8,64,128]{2,1,0:T(8,128)(2,1)S(1)}, u32[]{:S(2)}, u32[]{:S(2)}) async-start(bf16[8,64,128]{2,1,0:T(8,128)(2,1)} %bitcast.48), calls=%async_computation.7 | async-start | bytes 262144 | tf_op jit(solution)/shard_map/all_to_all | solution.py:155
  165.2 6.4 %fusion.22 = bf16[512,8,512]{0,2,1:T(8,128)(2,1)} fusion(f32[512,512,8]{1,0,2:T(8,128)} %copy-done.1, f32[512,8]{0,1:T(8,128)S(1)} %get-tuple-element.18, f32[512,8]{0,1:T(8,128)S(1)} %copy-done.12, pred[512,512]{0,1:T(8,128)(4,1)S(1)} %get-tuple-element.12, bf16[512,128,1]{1,0,2:T(8,128)(2,1)S(1)} %bitcast.299, bf16[512,8,128]{2,1,0:T(8,128)(2,1)S(1)} %bitcast.294), kind=kOutput, calls=%fused_computation.32 | convolution fusion | flops 549453824 | bytes 14057472 | tf_op jit(solution)/shard_map/thgd,shd->thgs/dot_general | solution.py:108
  171.6 4.1 %add_convert_fusion.1 = bf16[512,128]{1,0:T(8,128)(2,1)} fusion(bf16[512,128]{1,0:T(8,128)(2,1)S(1)} %collective-permute-done.2, bf16[512,8,512]{0,2,1:T(8,128)(2,1)} %fusion.22, bf16[512,8,128]{2,1,0:T(8,128)(2,1)S(1)} %bitcast.282), kind=kOutput, calls=%fused_computation.77 | convolution fusion | flops 537133056 | bytes 5505024 | tf_op jit(solution)/shard_map/thgs,thgd->shd/dot_general | solution.py:118
  175.7 5.1 %all-to-all-start.6 = ((bf16[8,64,128]{2,1,0:T(8,128)(2,1)}), bf16[8,64,128]{2,1,0:T(8,128)(2,1)S(1)}, u32[]{:S(2)}, u32[]{:S(2)}) async-start(bf16[8,64,128]{2,1,0:T(8,128)(2,1)} %bitcast.42), calls=%async_computation.6 | async-start | bytes 262144 | tf_op jit(solution)/shard_map/all_to_all | solution.py:154
  180.8 1.7 copy.110
  182.5 1.3 all_to_all.113
  183.8 3.8 %all-to-all-done.6 = bf16[8,64,128]{2,1,0:T(8,128)(2,1)S(1)} async-done(((bf16[8,64,128]{2,1,0:T(8,128)(2,1)}), bf16[8,64,128]{2,1,0:T(8,128)(2,1)S(1)}, u32[]{:S(2)}, u32[]{:S(2)}) %all-to-all-start.6) | async-done | bytes 131104 | tf_op jit(solution)/shard_map/all_to_all | solution.py:154
  187.5 3.6 %all-to-all-start.3 = ((bf16[8,64,1024]{2,1,0:T(8,128)(2,1)}), bf16[8,64,1024]{2,1,0:T(8,128)(2,1)S(1)}, u32[]{:S(2)}, u32[]{:S(2)}) async-start(bf16[8,64,1024]{2,1,0:T(8,128)(2,1)} %all_to_all.113), calls=%async_computation.3 | async-start | bytes 2097152 | tf_op jit(solution)/shard_map/all_to_all | solution.py:94
  191.1 3.5 %fusion.91 = f32[512,8,128]{2,0,1:T(8,128)S(1)} fusion(bf16[512,8,512]{0,2,1:T(8,128)(2,1)} %fusion.22, bf16[512,128,1]{1,0,2:T(8,128)(2,1)} %bitcast.3), kind=kOutput, calls=%fused_computation.111 | convolution fusion | flops 536870912 | bytes 6422528 | tf_op jit(solution)/shard_map/thgs,shd->thgd/dot_general | solution.py:114
  194.6 3.5 %fusion.43 = bf16[512,1,8,128]{3,0,2,1:T(8,128)(2,1)S(1)} fusion(f32[512,8,128]{2,0,1:T(8,128)S(1)} %fusion.91, bf16[512,8,512]{0,2,1:T(8,128)(2,1)} %copy-done.3, bf16[512,128]{1,0:T(8,128)(2,1)} %collective-permute-done), kind=kOutput, calls=%fused_computation.51 | convolution fusion | flops 538443776 | bytes 7471104 | tf_op jit(solution)/shard_map/thgs,shd->thgd/dot_general | solution.py:114
  198.1 0.7 copy.119
  198.8 1.3 all_to_all.120
  200.1 17.6 %all-to-all-done.3 = bf16[8,64,1024]{2,1,0:T(8,128)(2,1)S(1)} async-done(((bf16[8,64,1024]{2,1,0:T(8,128)(2,1)}), bf16[8,64,1024]{2,1,0:T(8,128)(2,1)S(1)}, u32[]{:S(2)}, u32[]{:S(2)}) %all-to-all-start.3) | async-done | bytes 1048608 | tf_op jit(solution)/shard_map/all_to_all | solution.py:94
  217.6 3.6 %all-to-all-start.5 = ((bf16[8,64,1024]{2,1,0:T(8,128)(2,1)}), bf16[8,64,1024]{2,1,0:T(8,128)(2,1)S(1)}, u32[]{:S(2)}, u32[]{:S(2)}) async-start(bf16[8,64,1024]{2,1,0:T(8,128)(2,1)} %all_to_all.120), calls=%async_computation.5 | async-start | bytes 2097152 | tf_op jit(solution)/shard_map/all_to_all | solution.py:153
  221.2 0.7 copy_bitcast_fusion.2
  221.9 0.7 copy_bitcast_fusion.3
  222.5 1.1 copy.139
  223.6 24.1 %all-to-all-done.5 = bf16[8,64,1024]{2,1,0:T(8,128)(2,1)S(1)} async-done(((bf16[8,64,1024]{2,1,0:T(8,128)(2,1)}), bf16[8,64,1024]{2,1,0:T(8,128)(2,1)S(1)}, u32[]{:S(2)}, u32[]{:S(2)}) %all-to-all-start.5) | async-done | bytes 1048608 | tf_op jit(solution)/shard_map/all_to_all | solution.py:153
  247.7 1.1 copy.140
  (28 shorter events, 0.1 us)
Async XLA Ops:
  0.6 0.9 copy-start
  1.5 57.2 %copy-start.13 = (s32[128]{0:T(128)S(1)}, s32[128]{0:T(128)}, u32[]{:S(2)}) copy-start(s32[128]{0:T(128)} %param.9) | copy-start | bytes 1540
  2.2 12.8 %all-to-all-start = ((bf16[64,8,128]{2,0,1:T(8,128)(2,1)}), bf16[64,8,128]{2,0,1:T(8,128)(2,1)}, u32[]{:S(2)}, u32[]{:S(2)}) async-start(bf16[64,8,128]{2,0,1:T(8,128)(2,1)} %copy_bitcast_fusion.5), calls=%async_computation | async-start | bytes 262144 | tf_op jit(solution)/shard_map/all_to_all | solution.py:26
  15.0 10.1 %all-to-all-start.2 = ((bf16[64,8,128]{2,0,1:T(8,128)(2,1)}), bf16[64,8,128]{2,0,1:T(8,128)(2,1)S(1)}, u32[]{:S(2)}, u32[]{:S(2)}) async-start(bf16[64,8,128]{2,0,1:T(8,128)(2,1)} %copy_bitcast_fusion.4), calls=%async_computation.2 | async-start | bytes 262144 | tf_op jit(solution)/shard_map/all_to_all | solution.py:27
  25.1 52.9 %copy-start.8 = (bf16[64,8,128]{2,0,1:T(8,128)(2,1)}, bf16[64,8,128]{2,0,1:T(8,128)(2,1)S(1)}, u32[]{:S(2)}) copy-start(bf16[64,8,128]{2,0,1:T(8,128)(2,1)S(1)} %all-to-all-done.2) | copy-start | bytes 393220
  25.1 30.1 %all-to-all-start.1 = ((bf16[64,8,1024]{2,0,1:T(8,128)(2,1)}), bf16[64,8,1024]{2,0,1:T(8,128)(2,1)S(1)}, u32[]{:S(2)}, u32[]{:S(2)}) async-start(bf16[64,8,1024]{2,0,1:T(8,128)(2,1)} %bitcast.278), calls=%async_computation.1 | async-start | bytes 2097152 | tf_op jit(solution)/shard_map/all_to_all | solution.py:25
  55.2 30.1 %all-to-all-start.4 = ((bf16[64,8,1024]{2,0,1:T(8,128)(2,1)}), bf16[64,8,1024]{2,0,1:T(8,128)(2,1)S(1)}, u32[]{:S(2)}, u32[]{:S(2)}) async-start(bf16[64,8,1024]{2,0,1:T(8,128)(2,1)} %bitcast.277), calls=%async_computation.4 | async-start | bytes 2097152 | tf_op jit(solution)/shard_map/all_to_all | solution.py:28
  59.6 43.6 %collective-permute-start = (bf16[512,128]{1,0:T(8,128)(2,1)}, bf16[512,128]{1,0:T(8,128)(2,1)}, u32[]{:S(2)}, u32[]{:S(2)}) collective-permute-start(bf16[512,128]{1,0:T(8,128)(2,1)} %bitcast.2), channel_id=1, source_target_pairs={{0,8},{8,16},{16,24},{24,32},{32,40},{40,48},{48,56},{56,64},{64,7... | collective-permute-start | bytes 393224 | tf_op jit(solution)/shard_map/ppermute | solution.py:15
  70.9 55.3 %collective-permute-start.1 = (bf16[512,128]{0,1:T(8,128)(2,1)}, bf16[512,128]{0,1:T(8,128)(2,1)}, u32[]{:S(2)}, u32[]{:S(2)}) collective-permute-start(bf16[512,128]{0,1:T(8,128)(2,1)} %copy.108), channel_id=1, source_target_pairs={{0,8},{8,16},{16,24},{24,32},{32,40},{40,48},{48,56},{56,64},{64,7... | collective-permute-start | bytes 393224 | tf_op jit(solution)/shard_map/ppermute | solution.py:15
  78.3 27.5 %copy-start.4 = (pred[512,512]{0,1:T(8,128)(4,1)S(1)}, pred[512,512]{0,1:T(8,128)(4,1)}, u32[]{:S(2)}) copy-start(pred[512,512]{0,1:T(8,128)(4,1)} %get-tuple-element.13) | copy-start | bytes 786436
  85.5 27.0 %copy-start.6 = (bf16[64,8,8,128]{3,2,1,0:T(8,128)(2,1)}, bf16[64,8,8,128]{3,2,1,0:T(8,128)(2,1)S(1)}, u32[]{:S(2)}) copy-start(bf16[64,8,8,128]{3,2,1,0:T(8,128)(2,1)S(1)} %copy.144) | copy-start | bytes 3145732
  105.8 6.8 %copy-start.2 = (f32[512,512,8]{1,0,2:T(8,128)}, f32[512,512,8]{1,0,2:T(8,128)S(1)}, u32[]{:S(2)}) copy-start(f32[512,512,8]{1,0,2:T(8,128)S(1)} %get-tuple-element.15) | copy-start | bytes 25165828
  110.2 10.3 %copy-start.1 = (f32[512,512,8]{1,0,2:T(8,128)}, f32[512,512,8]{1,0,2:T(8,128)S(1)}, u32[]{:S(2)}) copy-start(f32[512,512,8]{1,0,2:T(8,128)S(1)} %get-tuple-element.17) | copy-start | bytes 25165828
  111.9 8.5 %copy-start.9 = (bf16[64,8,128]{2,0,1:T(8,128)(2,1)S(1)}, bf16[64,8,128]{2,0,1:T(8,128)(2,1)}, u32[]{:S(2)}) copy-start(bf16[64,8,128]{2,0,1:T(8,128)(2,1)} %copy-done.8) | copy-start | bytes 393220
  112.6 11.0 %copy-start.11 = (f32[512,8]{0,1:T(8,128)}, f32[512,8]{0,1:T(8,128)S(1)}, u32[]{:S(2)}) copy-start(f32[512,8]{0,1:T(8,128)S(1)} %get-tuple-element.6) | copy-start | bytes 49156
  114.9 30.6 %collective-permute-start.3 = (bf16[512,128]{1,0:T(8,128)(2,1)}, bf16[512,128]{1,0:T(8,128)(2,1)}, u32[]{:S(2)}, u32[]{:S(2)}) collective-permute-start(bf16[512,128]{1,0:T(8,128)(2,1)} %fusion.55), channel_id=1, source_target_pairs={{8,0},{16,8},{24,16},{32,24},{40,32},{48,40},{56,48},{64,56},{72,6... | collective-permute-start | bytes 393224 | tf_op jit(solution)/shard_map/ppermute | solution.py:15
  126.2 8.2 %copy-start.5 = (pred[512,512]{0,1:T(8,128)(4,1)S(1)}, pred[512,512]{0,1:T(8,128)(4,1)}, u32[]{:S(2)}) copy-start(pred[512,512]{0,1:T(8,128)(4,1)} %get-tuple-element.13) | copy-start | bytes 786436
  126.2 8.2 %copy-start.7 = (bf16[64,8,8,128]{3,2,1,0:T(8,128)(2,1)S(1)}, bf16[64,8,8,128]{3,2,1,0:T(8,128)(2,1)}, u32[]{:S(2)}) copy-start(bf16[64,8,8,128]{3,2,1,0:T(8,128)(2,1)} %copy-done.6) | copy-start | bytes 3145732
  126.2 8.2 %copy-start.12 = (f32[512,8]{0,1:T(8,128)S(1)}, f32[512,8]{0,1:T(8,128)}, u32[]{:S(2)}) copy-start(f32[512,8]{0,1:T(8,128)} %copy-done.11) | copy-start | bytes 49156
  139.6 2.0 copy-start.3
  142.8 22.4 %copy-start.10 = (bf16[64,8,128]{2,0,1:T(8,128)(2,1)S(1)}, bf16[64,8,128]{2,0,1:T(8,128)(2,1)}, u32[]{:S(2)}) copy-start(bf16[64,8,128]{2,0,1:T(8,128)(2,1)} %copy-done.8) | copy-start | bytes 393220
  142.8 28.8 %collective-permute-start.2 = (bf16[512,128]{1,0:T(8,128)(2,1)S(1)}, bf16[512,128]{1,0:T(8,128)(2,1)S(1)}, u32[]{:S(2)}, u32[]{:S(2)}) collective-permute-start(bf16[512,128]{1,0:T(8,128)(2,1)S(1)} %fusion.58), channel_id=1, source_target_pairs={{8,0},{16,8},{24,16},{32,24},{40,32},{48,40},{56,48},{64,56},{72,6... | collective-permute-start | bytes 393224 | tf_op jit(solution)/shard_map/ppermute | solution.py:15
  151.4 24.3 %all-to-all-start.7 = ((bf16[8,64,128]{2,1,0:T(8,128)(2,1)}), bf16[8,64,128]{2,1,0:T(8,128)(2,1)S(1)}, u32[]{:S(2)}, u32[]{:S(2)}) async-start(bf16[8,64,128]{2,1,0:T(8,128)(2,1)} %bitcast.48), calls=%async_computation.7 | async-start | bytes 262144 | tf_op jit(solution)/shard_map/all_to_all | solution.py:155
  175.7 11.9 %all-to-all-start.6 = ((bf16[8,64,128]{2,1,0:T(8,128)(2,1)}), bf16[8,64,128]{2,1,0:T(8,128)(2,1)S(1)}, u32[]{:S(2)}, u32[]{:S(2)}) async-start(bf16[8,64,128]{2,1,0:T(8,128)(2,1)} %bitcast.42), calls=%async_computation.6 | async-start | bytes 262144 | tf_op jit(solution)/shard_map/all_to_all | solution.py:154
  187.5 30.1 %all-to-all-start.3 = ((bf16[8,64,1024]{2,1,0:T(8,128)(2,1)}), bf16[8,64,1024]{2,1,0:T(8,128)(2,1)S(1)}, u32[]{:S(2)}, u32[]{:S(2)}) async-start(bf16[8,64,1024]{2,1,0:T(8,128)(2,1)} %all_to_all.113), calls=%async_computation.3 | async-start | bytes 2097152 | tf_op jit(solution)/shard_map/all_to_all | solution.py:94
  217.6 30.1 %all-to-all-start.5 = ((bf16[8,64,1024]{2,1,0:T(8,128)(2,1)}), bf16[8,64,1024]{2,1,0:T(8,128)(2,1)S(1)}, u32[]{:S(2)}, u32[]{:S(2)}) async-start(bf16[8,64,1024]{2,1,0:T(8,128)(2,1)} %all_to_all.120), calls=%async_computation.5 | async-start | bytes 2097152 | tf_op jit(solution)/shard_map/all_to_all | solution.py:153
where the time goes:
time: 250 us; the launch traced here: 249 us
  waiting for transfers between devices  104 us (42%)
  starting transfers between devices  66.9 us (27%)
  matrix products  48.5 us (19%)
  local copies, waits for them, and re-layouts  22 us (9%)
  other arithmetic  6.44 us (3%)
    ppermute x4, starting transfers between devices, from_behind(): return lax.ppermute(block, axis, route)  24.5 us
    all_to_all x1, waiting for transfers between devices, per_device(): lax.all_to_all(queries, 'hd', split_axis=1, concat_axis=0, tiled=True)  24.2 us
    all_to_all x1, waiting for transfers between devices, per_device(): lax.all_to_all(query_local_grad, 'hd', split_axis=0, concat_axis=1, tiled...  24.1 us
    ppermute x4, waiting for transfers between devices, from_behind(): return lax.ppermute(block, axis, route)  17.6 us
    all_to_all x1, waiting for transfers between devices, per_device(): lax.all_to_all(out_heads.reshape(row_count, kv_heads * group_size * DH),...  17.6 us
    all_to_all x1, starting transfers between devices, per_device(): lax.all_to_all(value_local_grad, 'hd', split_axis=0, concat_axis=1, tiled...  13.8 us
    dot_general x2, matrix products, grads_for(): jnp.einsum('thgd,shd->thgs', grad_heads, value_heads, preferred_element_t...  11.5 us
    dot_general x2, matrix products, forward_step(): jnp.einsum('thgs,shd->thgd', weights.astype(jnp.bfloat16), value_heads, p...  11.2 us
  transfers between devices with their start and end apart: 12, of which 8 were waited for; matrix products, arithmetic and copies ran while one was open for 28% of the time, Pallas kernels for 0%

commit v1 on v0

v1 whole, which is shorter than its diff:
```python
import functools
import math

import jax
import jax.numpy as jnp
from jax import lax
from jax.experimental import pallas as pl
from jax.experimental.pallas import tpu as pltpu
from jax.sharding import PartitionSpec as P

DH = 128
ROWS = 64
CHIP = 2 * ROWS
SLOTS = 5
KEYS = SLOTS * CHIP
HEADS = 4
GROUP = 8
WIDE = GROUP * DH
PAIR = 2 * CHIP
SCALE = DH ** (-0.5)
MESH = pl.DeviceIdType.MESH
F32 = jnp.float32
BF16 = jnp.bfloat16


def kernel(
    devices,
    q_in, k_in, v_in, g_in, len_in,
    att_out, dq_out, dk_out, dv_out,
    kv, qb, gb, ob, dqb, acc, gin, gout, fin, bias, lens,
    key_pair, key_t, value_pair, value_t, scores, weights, probs, changes,
    len_sem, kv_recv, kv_fwd, own_ici, own_sib,
    qg_recv, qg_send, sum_recv, sum_send,
    out_loc, out_send, out_recv, fin_loc, fin_send, fin_recv,
):
    cp = lax.axis_index("cp")
    hd = lax.axis_index("hd")
    me = cp * 8 + hd
    core = lax.rem(hd, 2)
    other = 1 - core

    def device(index):
        index = lax.rem(index + devices, devices)
        return (index // 8, lax.rem(index, 8))

    sibling = (cp, hd + 1 - 2 * core)
    chip_base = me - core
    ahead = device(me + 2)
    ahead_other = device(chip_base + 2 + other)
    behind = device(me - 2)
    behind_other = device(chip_base - 2 + other)
    my_rows = pl.ds(pl.multiple_of(core * ROWS, ROWS), ROWS)
    sib_rows = pl.ds(pl.multiple_of(other * ROWS, ROWS), ROWS)

    def head_cols(owner, h, width):
        return pl.ds(pl.multiple_of((owner * HEADS + h) * width, width), width)

    def remote(src, dst, send, recv, target):
        return pltpu.make_async_remote_copy(
            src_ref=src, dst_ref=dst, send_sem=send, recv_sem=recv, device_id=target, device_id_type=MESH
        )

    def own_to_ahead(h):
        made = []
        for side, (owner, target) in enumerate(((core, ahead), (other, ahead_other))):
            for part, src in enumerate((k_in, v_in)):
                made.append(remote(
                    src.at[:, head_cols(owner, h, DH)], kv.at[h, 3, part, my_rows],
                    own_ici.at[h, side, part], kv_recv.at[h, 3], target,
                ))
        return made

    def own_to_sibling(h):
        return [
            remote(src.at[:, head_cols(other, h, DH)], kv.at[h, 4, part, my_rows],
                   own_sib.at[h, part], kv_recv.at[h, 4], sibling)
            for part, src in enumerate((k_in, v_in))
        ]

    def own_local(h):
        return [
            pltpu.make_async_copy(src.at[:, head_cols(core, h, DH)], kv.at[h, 4, part, my_rows], kv_recv.at[h, 4])
            for part, src in enumerate((k_in, v_in))
        ]

    def rows_to_sibling(h):
        return [
            remote(src.at[:, head_cols(other, h, WIDE)], dst.at[h, my_rows],
                   qg_send.at[h, part], qg_recv.at[h, part], sibling)
            for part, (src, dst) in enumerate(((q_in, qb), (g_in, gb)))
        ]

    def rows_local(h):
        return [
            pltpu.make_async_copy(src.at[:, head_cols(core, h, WIDE)], dst.at[h, my_rows], qg_recv.at[h, part])
            for part, (src, dst) in enumerate(((q_in, qb), (g_in, gb)))
        ]

    def start(copies):
        for copy in copies:
            copy.start()

    def wait_kv(h, slot):
        pltpu.make_async_copy(kv.at[h, slot], kv.at[h, slot], kv_recv.at[h, slot]).wait()

    def wait_rows(h):
        for part, dst in enumerate((qb, gb)):
            pltpu.make_async_copy(dst.at[h], dst.at[h], qg_recv.at[h, part]).wait()

    def forward(h, slot):
        return remote(kv.at[h, slot], kv.at[h, slot - 1], kv_fwd.at[h, slot - 1], kv_recv.at[h, slot - 1], ahead)

    def own_ahead(h):
        start(own_to_ahead(h))

    def pass_on(h, slot):
        wait_kv(h, slot)
        forward(h, slot).start()

    def sum_copy(h, slot):
        return remote(gout.at[h, slot], gin.at[h, slot], sum_send.at[h, slot], sum_recv.at[h, slot], behind)

    def first_sum(h):
        for part in range(2):
            gout[h, 0, part] = acc[h, part, 0:CHIP].astype(BF16)
        sum_copy(h, 0).start()

    def next_sum(h, slot):
        pltpu.make_async_copy(gin.at[h, slot - 1], gin.at[h, slot - 1], sum_recv.at[h, slot - 1]).wait()
        for part in range(2):
            total = gin[h, slot - 1, part].astype(F32) + acc[h, part, slot * CHIP:(slot + 1) * CHIP]
            if slot < 4:
                gout[h, slot, part] = total.astype(BF16)
            else:
                fin[h, part] = total.astype(BF16)
        if slot < 4:
            sum_copy(h, slot).start()
        else:
            start(fin_local(h))
            start(fin_remote(h))

    def fin_local(h):
        return [
            pltpu.make_async_copy(fin.at[h, part, my_rows], dst.at[:, head_cols(core, h, DH)], fin_loc.at[h, part])
            for part, dst in enumerate((dk_out, dv_out))
        ]

    def fin_remote(h):
        return [
            remote(fin.at[h, part, sib_rows], dst.at[:, head_cols(core, h, DH)],
                   fin_send.at[h, part], fin_recv.at[h, part], sibling)
            for part, dst in enumerate((dk_out, dv_out))
        ]

    def out_local(h):
        return [
            pltpu.make_async_copy(src.at[h, my_rows], dst.at[:, head_cols(core, h, WIDE)], out_loc.at[h, part])
            for part, (src, dst) in enumerate(((ob, att_out), (dqb, dq_out)))
        ]

    def out_remote(h):
        return [
            remote(src.at[h, sib_rows], dst.at[:, head_cols(core, h, WIDE)],
                   out_send.at[h, part], out_recv.at[h, part], sibling)
            for part, (src, dst) in enumerate(((ob, att_out), (dqb, dq_out)))
        ]

    barrier = pltpu.get_barrier_semaphore()
    for peer in (sibling, ahead, ahead_other, behind, behind_other):
        pl.semaphore_signal(barrier, inc=1, device_id=peer, device_id_type=MESH)
    len_copy = pltpu.make_async_copy(len_in, lens, len_sem)
    len_copy.start()
    for h in range(HEADS):
        start(own_local(h))
    for h in range(HEADS):
        start(rows_local(h))
    pl.semaphore_wait(barrier, 5)

    start(own_to_ahead(0))
    start(own_to_ahead(1))
    for h in range(HEADS):
        start(own_to_sibling(h))
    start(rows_to_sibling(0))

    len_copy.wait()
    first_pos = (chip_base // 2) * CHIP
    low = lax.broadcasted_iota(jnp.int32, (DH, DH), 0)
    high = lax.broadcasted_iota(jnp.int32, (DH, DH), 1)
    ends_col = jnp.sum(jnp.where(high <= low, lens[...].astype(F32), 0.0), axis=1, keepdims=True)
    ends_row = jnp.sum(jnp.where(low == high, ends_col, 0.0), axis=0, keepdims=True)
    query_pos = high + first_pos
    query_seg = jnp.sum(jnp.where(ends_col <= query_pos.astype(F32), 1.0, 0.0), axis=0, keepdims=True)
    for slot in range(SLOTS):
        key_pos = low + (first_pos - (4 - slot) * CHIP)
        key_seg = jnp.sum(jnp.where(ends_row <= key_pos.astype(F32), 1.0, 0.0), axis=1, keepdims=True)
        allowed = (key_pos >= 0) & (key_pos <= query_pos) & (key_seg == query_seg)
        bias[slot * CHIP:(slot + 1) * CHIP, :] = jnp.where(allowed, 0.0, -1e30)

    pass_on(0, 3)
    start(rows_to_sibling(1))
    pass_on(1, 3)
    pass_on(0, 2)
    start(rows_to_sibling(2))
    pass_on(1, 2)
    pass_on(0, 1)
    start(own_to_ahead(2))
    start(rows_to_sibling(3))
    pass_on(1, 1)

    lane = lax.broadcasted_iota(jnp.int32, (PAIR, DH), 1)
    key_lane = lax.broadcasted_iota(jnp.int32, (KEYS, DH), 1)
    value_pair[:, DH:] = jnp.where(key_lane < 2, -1.0, 0.0).astype(BF16)
    value_t[DH:, :] = jnp.ones((16, KEYS), BF16)
    blocks = [slice(slot * CHIP, (slot + 1) * CHIP) for slot in range(SLOTS)]
    across = (((1,), (1,)), ((), ()))

    def prepare(h):
        keys = kv[h, :, 0].reshape(KEYS, DH)
        values = kv[h, :, 1].reshape(KEYS, DH)
        key_t[...] = keys.T
        value_t[:DH, :] = values.T
        value_pair[:, :DH] = values
        scaled = keys.astype(F32) * (SCALE * math.log2(math.e))
        scaled_top = scaled.astype(BF16)
        key_pair[:, :DH] = scaled_top
        key_pair[:, DH:] = (scaled - scaled_top.astype(F32)).astype(BF16)

    def chunk(h, p):
        cols = [slice((2 * p + i) * DH, (2 * p + i + 1) * DH) for i in range(2)]
        pair = slice(p * PAIR, (p + 1) * PAIR)
        query = jnp.concatenate([qb[h, :, c] for c in cols], axis=0)
        query = jnp.concatenate([query, query], axis=1)
        top = None
        for block in blocks:
            one_bias = bias[block]
            part = lax.dot_general(key_pair[block], query, across, preferred_element_type=F32)
            part = part + jnp.concatenate([one_bias, one_bias], axis=1)
            scores[block] = part
            part = jnp.max(part.reshape(CHIP // 8, 8, PAIR), axis=0)
            top = part if top is None else jnp.maximum(top, part)
        top = jnp.max(top, axis=0, keepdims=True)
        for block in blocks:
            weights[block] = jnp.exp2(scores[block] - top).astype(BF16)
        out = jnp.dot(value_t[...], weights[...], preferred_element_type=F32)
        inverse = 1.0 / out[DH:DH + 1]
        out = (out[:DH] * inverse).T.astype(BF16)
        grad = jnp.concatenate([gb[h, :, c] for c in cols], axis=0)
        for i, c in enumerate(cols):
            ob[h, :, c] = out[i * CHIP:(i + 1) * CHIP]
        delta = jnp.sum(out.astype(F32) * grad.astype(F32), axis=1, keepdims=True)
        delta_top = delta.astype(BF16).astype(F32)
        tail = jnp.where(lane == 0, delta_top, jnp.where(lane == 1, delta - delta_top, 0.0)).astype(BF16)
        grad = jnp.concatenate([grad, tail], axis=1)
        inverse = jnp.broadcast_to(inverse, (CHIP, PAIR)).astype(BF16)
        for block in blocks:
            change = lax.dot_general(value_pair[block], grad, across, preferred_element_type=F32).astype(BF16)
            prob = weights[block] * inverse
            probs[block, pair] = prob
            changes[block, pair] = prob * change
        query_grad = (jnp.dot(key_t[...], changes[:, pair], preferred_element_type=F32) * SCALE).T.astype(BF16)
        for i, c in enumerate(cols):
            dqb[h, :, c] = query_grad[i * CHIP:(i + 1) * CHIP]

    def key_sums(h):
        query = jnp.concatenate([qb[h, :, g * DH:(g + 1) * DH] for g in range(GROUP)], axis=0)
        acc[h, 0] = jnp.dot(changes[...], query, preferred_element_type=F32) * SCALE
        grad = jnp.concatenate([gb[h, :, g * DH:(g + 1) * DH] for g in range(GROUP)], axis=0)
        acc[h, 1] = jnp.dot(probs[...], grad, preferred_element_type=F32)

    after = {
        (0, 1): [(pass_on, 2, 3), (own_ahead, 3)],
        (0, 3): [(pass_on, 2, 2)],
        (1, 0): [(pass_on, 3, 3)],
        (1, 2): [(pass_on, 2, 1)],
        (1, 3): [(pass_on, 3, 2), (next_sum, 0, 1)],
        (2, 0): [(pass_on, 3, 1)],
        (2, 1): [(next_sum, 0, 2)],
        (2, 2): [(next_sum, 1, 1)],
        (2, 3): [(next_sum, 0, 3)],
        (3, 0): [(next_sum, 1, 2)],
        (3, 1): [(next_sum, 0, 4)],
        (3, 2): [(next_sum, 2, 1)],
        (3, 3): [(next_sum, 1, 3)],
    }
    for h in range(HEADS):
        wait_rows(h)
        wait_kv(h, 4)
        wait_kv(h, 0)
        prepare(h)
        for p in range(GROUP // 2):
            chunk(h, p)
            if p == GROUP // 2 - 1:
                key_sums(h)
                first_sum(h)
                start(out_remote(h))
                start(out_local(h))
            for event, *where in after.get((h, p), []):
                event(*where)
    for h, slot in ((2, 2), (3, 1), (1, 4), (2, 3), (3, 2), (2, 4), (3, 3), (3, 4)):
        next_sum(h, slot)

    for h in range(HEADS):
        for copy in own_to_ahead(h) + own_to_sibling(h) + rows_to_sibling(h):
            copy.wait_send()
        for slot in (3, 2, 1):
            forward(h, slot).wait_send()
        for slot in range(4):
            sum_copy(h, slot).wait_send()
        for copy in out_local(h) + fin_local(h):
            copy.wait()
        for copy in out_remote(h) + fin_remote(h):
            copy.wait_send()
        for part, dst in enumerate((att_out, dq_out)):
            ref = dst.at[:, head_cols(other, h, WIDE)]
            pltpu.make_async_copy(ref, ref, out_recv.at[h, part]).wait()
        for part, dst in enumerate((dk_out, dv_out)):
            ref = dst.at[:, head_cols(other, h, DH)]
            pltpu.make_async_copy(ref, ref, fin_recv.at[h, part]).wait()


def copy_out(*refs):
    sources, targets, sem = refs[:4], refs[4:8], refs[8]
    copies = []
    for src, dst in zip(sources, targets):
        pieces = 4 if src.shape[1] > 1024 else 1
        step = src.shape[0] // pieces
        for piece in range(pieces):
            rows = pl.ds(piece * step, step)
            copies.append(pltpu.make_async_copy(src.at[rows], dst.at[rows], sem.at[len(copies)]))
    for copy in copies:
        copy.start()
    for copy in copies:
        copy.wait()


def solution(mesh):
    devices = mesh.shape["cp"] * mesh.shape["hd"]
    anywhere = pl.BlockSpec(memory_space=pl.ANY)
    dma = pltpu.SemaphoreType.DMA

    def per_device(queries, key_vectors, value_vectors, out_grad, doc_lengths):
        wide = jax.ShapeDtypeStruct(queries.shape, BF16)
        narrow = jax.ShapeDtypeStruct(key_vectors.shape, BF16)
        results = pl.pallas_call(
            functools.partial(kernel, devices),
            out_shape=(wide, wide, narrow, narrow),
            in_specs=[anywhere] * 5,
            out_specs=(anywhere,) * 4,
            scratch_shapes=[
                pltpu.VMEM((HEADS, SLOTS, 2, CHIP, DH), BF16),
                pltpu.VMEM((HEADS, CHIP, WIDE), BF16),
                pltpu.VMEM((HEADS, CHIP, WIDE), BF16),
                pltpu.VMEM((HEADS, CHIP, WIDE), BF16),
                pltpu.VMEM((HEADS, CHIP, WIDE), BF16),
                pltpu.VMEM((HEADS, 2, KEYS, DH), F32),
                pltpu.VMEM((HEADS, 4, 2, CHIP, DH), BF16),
                pltpu.VMEM((HEADS, 4, 2, CHIP, DH), BF16),
                pltpu.VMEM((HEADS, 2, CHIP, DH), BF16),
                pltpu.VMEM((KEYS, DH), F32),
                pltpu.VMEM((1, 128), jnp.int32),
                pltpu.VMEM((KEYS, 2 * DH), BF16),
                pltpu.VMEM((DH, KEYS), BF16),
                pltpu.VMEM((KEYS, 2 * DH), BF16),
                pltpu.VMEM((DH + 16, KEYS), BF16),
                pltpu.VMEM((KEYS, PAIR), F32),
                pltpu.VMEM((KEYS, PAIR), BF16),
                pltpu.VMEM((KEYS, GROUP * CHIP), BF16),
                pltpu.VMEM((KEYS, GROUP * CHIP), BF16),
                dma,
                dma((HEADS, SLOTS)),
                dma((HEADS, 3)),
                dma((HEADS, 2, 2)),
                dma((HEADS, 2)),
                dma((HEADS, 2)),
                dma((HEADS, 2)),
                dma((HEADS, 4)),
                dma((HEADS, 4)),
                dma((HEADS, 2)),
                dma((HEADS, 2)),
                dma((HEADS, 2)),
                dma((HEADS, 2)),
                dma((HEADS, 2)),
                dma((HEADS, 2)),
            ],
            compiler_params=pltpu.CompilerParams(
                collective_id=0, has_side_effects=True, vmem_limit_bytes=56 * 1024 * 1024
            ),
            cost_estimate=pl.CostEstimate(
                flops=HEADS * GROUP * CHIP * KEYS * DH * 12,
                bytes_accessed=5 * 1024 * 1024,
                transcendentals=HEADS * GROUP * CHIP * KEYS,
            ),
        )(queries, key_vectors, value_vectors, out_grad, doc_lengths.reshape(1, -1))
        return pl.pallas_call(
            copy_out,
            out_shape=(wide, wide, narrow, narrow),
            in_specs=[pl.BlockSpec(memory_space=pltpu.HBM)] * 4,
            out_specs=(anywhere,) * 4,
            scratch_shapes=[dma((10,))],
        )(*results)

    token = P(("cp", "hd"), None)
    return jax.shard_map(
        per_device,
        mesh=mesh,
        in_specs=(token, token, token, token, P()),
        out_specs=(token,) * 4,
        check_vma=False,
    )
```

time: 250 us -> 151 us (0.60)
  the two profiles are of different devices: /device:TPU:6 before, /device:TPU:1 now
where the time goes in v1:
time: 151 us
  Pallas kernels  151 us (100%)
    pallas_call x1, Pallas kernels, per_device(): pl.pallas_call(functools.partial(kernel, devices), out_shape=(wide, wide,...  77.9 us
    pallas_call x1, Pallas kernels, per_device(): pl.pallas_call(copy_out, out_shape=(wide, wide, narrow, narrow), in_specs...  72.7 us

profile of v1, /device:TPU:1, one launch (start us, length us, event | category | flops | bytes accessed | tf_op | source)
XLA Modules:
  0.0 151.3 jit_solution(9813877302809054722)
XLA Ops:
  0.6 77.9 %shard_map.84 = (bf16[64,8192]{1,0:T(8,128)(2,1)}, bf16[64,8192]{1,0:T(8,128)(2,1)}, bf16[64,1024]{1,0:T(8,128)(2,1)}, bf16[64,1024]{1,0:T(8,128)(2,1)}) custom-call(bf16[64,8192]{1,0:T(8,128)(2,1)} %q_in.1, bf16[64,1024]{1,0:T(8,128)(2,1)} %k_in.1, bf16[64,1024]{1,0:T(8,128)(2,1)} %v_in.1, bf16[64,8192]{1,0:T(8,128)(2,1)} %g_in.1, s32[1,128]{1,0:T(1,128)} %bitcast.1), custom_call_target="tpu_custom_call" | custom-call | flops 4026531840 | bytes 5242880 | tf_op jit(solution)/shard_map/pallas_call | solution.py:344
  78.5 72.7 %shard_map.85 = (bf16[64,8192]{1,0:T(8,128)(2,1)}, bf16[64,8192]{1,0:T(8,128)(2,1)}, bf16[64,1024]{1,0:T(8,128)(2,1)}, bf16[64,1024]{1,0:T(8,128)(2,1)}) custom-call(bf16[64,8192]{1,0:T(8,128)(2,1)} %get-tuple-element.8.refs_0_, bf16[64,8192]{1,0:T(8,128)(2,1)} %get-tuple-element.9.refs_1_, bf16[64,1024]{1,0:T(8,128)(2,1)} %get-tuple-element.10.refs_2_, ...), custom_call_target="tpu_custom_call" | custom-call | tf_op jit(solution)/shard_map/pallas_call | solution.py:394

commit v2 on v1

--- a/solution.py
+++ b/solution.py
@@ -29,9 +29,10 @@
     att_out, dq_out, dk_out, dv_out,
     kv, qb, gb, ob, dqb, acc, gin, gout, fin, bias, lens,
     key_pair, key_t, value_pair, value_t, scores, weights, probs, changes,
+    k_own, v_own, q_away, g_away,
     len_sem, kv_recv, kv_fwd, own_ici, own_sib,
     qg_recv, qg_send, sum_recv, sum_send,
-    out_loc, out_send, out_recv, fin_loc, fin_send, fin_recv,
+    out_send, out_recv, fin_send, fin_recv, kv_stage, qg_stage,
 ):
     cp = lax.axis_index("cp")
     hd = lax.axis_index("hd")
@@ -63,7 +64,7 @@
     def own_to_ahead(h):
         made = []
         for side, (owner, target) in enumerate(((core, ahead), (other, ahead_other))):
-            for part, src in enumerate((k_in, v_in)):
+            for part, src in enumerate((k_own, v_own)):
                 made.append(remote(
                     src.at[:, head_cols(owner, h, DH)], kv.at[h, 3, part, my_rows],
                     own_ici.at[h, side, part], kv_recv.at[h, 3], target,
@@ -74,7 +75,7 @@
         return [
             remote(src.at[:, head_cols(other, h, DH)], kv.at[h, 4, part, my_rows],
                    own_sib.at[h, part], kv_recv.at[h, 4], sibling)
-            for part, src in enumerate((k_in, v_in))
+            for part, src in enumerate((k_own, v_own))
         ]
 
     def own_local(h):
@@ -85,10 +86,26 @@
 
     def rows_to_sibling(h):
         return [
-            remote(src.at[:, head_cols(other, h, WIDE)], dst.at[h, my_rows],
-                   qg_send.at[h, part], qg_recv.at[h, part], sibling)
-            for part, (src, dst) in enumerate(((q_in, qb), (g_in, gb)))
-        ]
+            remote(src.at[h], dst.at[h, my_rows], qg_send.at[h, part], qg_recv.at[h, part], sibling)
+            for part, (src, dst) in enumerate(((q_away, qb), (g_away, gb)))
+        ]
+
+    def stage_kv():
+        return [
+            pltpu.make_async_copy(src, dst, kv_stage.at[part])
+            for part, (src, dst) in enumerate(((k_in, k_own), (v_in, v_own)))
+        ]
+
+    def stage_rows(h):
+        return [
+            pltpu.make_async_copy(src.at[:, head_cols(other, h, WIDE)], dst.at[h], qg_stage.at[h, part])
+            for part, (src, dst) in enumerate(((q_in, q_away), (g_in, g_away)))
+        ]
+
+    def send_rows(h):
+        for copy in stage_rows(h):
+            copy.wait()
+        start(rows_to_sibling(h))
 
     def rows_local(h):
         return [
@@ -136,14 +153,12 @@
         if slot < 4:
             sum_copy(h, slot).start()
         else:
-            start(fin_local(h))
             start(fin_remote(h))
-
-    def fin_local(h):
-        return [
-            pltpu.make_async_copy(fin.at[h, part, my_rows], dst.at[:, head_cols(core, h, DH)], fin_loc.at[h, part])
-            for part, dst in enumerate((dk_out, dv_out))
-        ]
+            keep_fin(h)
+
+    def keep_fin(h):
+        for part, dst in enumerate((dk_out, dv_out)):
+            dst[:, head_cols(core, h, DH)] = fin[h, part, my_rows]
 
     def fin_remote(h):
         return [
@@ -152,11 +167,9 @@
             for part, dst in enumerate((dk_out, dv_out))
         ]
 
-    def out_local(h):
-        return [
-            pltpu.make_async_copy(src.at[h, my_rows], dst.at[:, head_cols(core, h, WIDE)], out_loc.at[h, part])
-            for part, (src, dst) in enumerate(((ob, att_out), (dqb, dq_out)))
-        ]
+    def keep_out(h):
+        for src, dst in ((ob, att_out), (dqb, dq_out)):
+            dst[:, head_cols(core, h, WIDE)] = src[h, my_rows]
 
     def out_remote(h):
         return [
@@ -170,17 +183,20 @@
         pl.semaphore_signal(barrier, inc=1, device_id=peer, device_id_type=MESH)
     len_copy = pltpu.make_async_copy(len_in, lens, len_sem)
     len_copy.start()
+    start(stage_kv())
     for h in range(HEADS):
         start(own_local(h))
-    for h in range(HEADS):
+        start(stage_rows(h))
         start(rows_local(h))
+    for copy in stage_kv():
+        copy.wait()
     pl.semaphore_wait(barrier, 5)
 
-    start(own_to_ahead(0))
-    start(own_to_ahead(1))
+    for h in range(3):
+        own_ahead(h)
     for h in range(HEADS):
         start(own_to_sibling(h))
-    start(rows_to_sibling(0))
+    send_rows(0)
 
     len_copy.wait()
     first_pos = (chip_base // 2) * CHIP
@@ -197,15 +213,14 @@
         bias[slot * CHIP:(slot + 1) * CHIP, :] = jnp.where(allowed, 0.0, -1e30)
 
     pass_on(0, 3)
-    start(rows_to_sibling(1))
-    pass_on(1, 3)
-    pass_on(0, 2)
-    start(rows_to_sibling(2))
-    pass_on(1, 2)
-    pass_on(0, 1)
-    start(own_to_ahead(2))
-    start(rows_to_sibling(3))
-    pass_on(1, 1)
+    own_ahead(3)
+    send_rows(1)
+    for h, slot in ((1, 3), (2, 3), (0, 2), (3, 3), (1, 2), (2, 2), (0, 1)):
+        pass_on(h, slot)
+    send_rows(2)
+    for h, slot in ((3, 2), (1, 1), (2, 1)):
+        pass_on(h, slot)
+    send_rows(3)
 
     lane = lax.broadcasted_iota(jnp.int32, (PAIR, DH), 1)
     key_lane = lax.broadcasted_iota(jnp.int32, (KEYS, DH), 1)
@@ -268,19 +283,14 @@
         acc[h, 1] = jnp.dot(probs[...], grad, preferred_element_type=F32)
 
     after = {
-        (0, 1): [(pass_on, 2, 3), (own_ahead, 3)],
-        (0, 3): [(pass_on, 2, 2)],
-        (1, 0): [(pass_on, 3, 3)],
-        (1, 2): [(pass_on, 2, 1)],
-        (1, 3): [(pass_on, 3, 2), (next_sum, 0, 1)],
-        (2, 0): [(pass_on, 3, 1)],
+        (0, 0): [(pass_on, 3, 1)],
+        (1, 2): [(next_sum, 0, 1)],
         (2, 1): [(next_sum, 0, 2)],
         (2, 2): [(next_sum, 1, 1)],
-        (2, 3): [(next_sum, 0, 3)],
-        (3, 0): [(next_sum, 1, 2)],
-        (3, 1): [(next_sum, 0, 4)],
+        (3, 0): [(next_sum, 0, 3)],
+        (3, 1): [(next_sum, 1, 2)],
         (3, 2): [(next_sum, 2, 1)],
-        (3, 3): [(next_sum, 1, 3)],
+        (3, 3): [(next_sum, 0, 4), (next_sum, 1, 3)],
     }
     for h in range(HEADS):
         wait_rows(h)
@@ -293,7 +303,7 @@
                 key_sums(h)
                 first_sum(h)
                 start(out_remote(h))
-                start(out_local(h))
+                keep_out(h)
             for event, *where in after.get((h, p), []):
                 event(*where)
     for h, slot in ((2, 2), (3, 1), (1, 4), (2, 3), (3, 2), (2, 4), (3, 3), (3, 4)):
@@ -306,8 +316,6 @@
             forward(h, slot).wait_send()
         for slot in range(4):
             sum_copy(h, slot).wait_send()
-        for copy in out_local(h) + fin_local(h):
-            copy.wait()
         for copy in out_remote(h) + fin_remote(h):
             copy.wait_send()
         for part, dst in enumerate((att_out, dq_out)):
@@ -343,9 +351,9 @@
         narrow = jax.ShapeDtypeStruct(key_vectors.shape, BF16)
         results = pl.pallas_call(
             functools.partial(kernel, devices),
-            out_shape=(wide, wide, narrow, narrow),
+            out_shape=tuple(pltpu.VMEM(x.shape, BF16) for x in (wide, wide, narrow, narrow)),
             in_specs=[anywhere] * 5,
-            out_specs=(anywhere,) * 4,
+            out_specs=(pl.BlockSpec(memory_space=pltpu.VMEM),) * 4,
             scratch_shapes=[
                 pltpu.VMEM((HEADS, SLOTS, 2, CHIP, DH), BF16),
                 pltpu.VMEM((HEADS, CHIP, WIDE), BF16),
@@ -366,6 +374,10 @@
                 pltpu.VMEM((KEYS, PAIR), BF16),
                 pltpu.VMEM((KEYS, GROUP * CHIP), BF16),
                 pltpu.VMEM((KEYS, GROUP * CHIP), BF16),
+                pltpu.VMEM((ROWS, 2 * HEADS * DH), BF16),
+                pltpu.VMEM((ROWS, 2 * HEADS * DH), BF16),
+                pltpu.VMEM((HEADS, ROWS, WIDE), BF16),
+                pltpu.VMEM((HEADS, ROWS, WIDE), BF16),
                 dma,
                 dma((HEADS, SLOTS)),
                 dma((HEADS, 3)),
@@ -379,7 +391,7 @@
                 dma((HEADS, 2)),
                 dma((HEADS, 2)),
                 dma((HEADS, 2)),
-                dma((HEADS, 2)),
+                dma((2,)),
                 dma((HEADS, 2)),
             ],
             compiler_params=pltpu.CompilerParams(
@@ -394,9 +406,10 @@
         return pl.pallas_call(
             copy_out,
             out_shape=(wide, wide, narrow, narrow),
-            in_specs=[pl.BlockSpec(memory_space=pltpu.HBM)] * 4,
+            in_specs=[pl.BlockSpec(memory_space=pltpu.VMEM)] * 4,
             out_specs=(anywhere,) * 4,
             scratch_shapes=[dma((10,))],
+            compiler_params=pltpu.CompilerParams(vmem_limit_bytes=8 * 1024 * 1024),
         )(*results)
 
     token = P(("cp", "hd"), None)

time: 151 us -> 78.4 us (0.52)
  Pallas kernels: 151 us -> 77.5 us
    pallas_call x1, Pallas kernels: 72.7 us -> 1.48 us  [per_device(): pl.pallas_call(copy_out, out_shape=(wide, wide, narrow, narrow), in_specs...]
    pallas_call x1, Pallas kernels: 77.9 us -> 76 us  [per_device(): pl.pallas_call(functools.partial(kernel, devices), out_shape=tuple((pltpu...]
where the time goes in v2:
time: 78.4 us; the launch traced here: 78.3 us
  Pallas kernels  77.5 us (99%)
  between operations  0.8 us (1%)
    pallas_call x1, Pallas kernels, per_device(): pl.pallas_call(functools.partial(kernel, devices), out_shape=tuple((pltpu...  76 us

profile of v2, /device:TPU:1, one launch (start us, length us, event | category | flops | bytes accessed | tf_op | source)
XLA Modules:
  0.0 78.3 jit_solution(11694632992371873965)
XLA Ops:
  0.6 76.0 %shard_map.84 = (bf16[64,8192]{1,0:T(8,128)(2,1)S(1)}, bf16[64,8192]{1,0:T(8,128)(2,1)S(1)}, bf16[64,1024]{1,0:T(8,128)(2,1)S(1)}, bf16[64,1024]{1,0:T(8,128)(2,1)S(1)}) custom-call(bf16[64,8192]{1,0:T(8,128)(2,1)} %q_in.1, bf16[64,1024]{1,0:T(8,128)(2,1)} %k_in.1, bf16[64,1024]{1,0:T(8,128)(2,1)} %v_in.1, bf16[64,8192]{1,0:T(8,128)(2,1)} %g_in.1, ...), custom_call_target="tpu_custom_call" | custom-call | flops 4026531840 | bytes 5242880 | tf_op jit(solution)/shard_map/pallas_call | solution.py:352
  76.6 1.5 %shard_map.85 = (bf16[64,8192]{1,0:T(8,128)(2,1)}, bf16[64,8192]{1,0:T(8,128)(2,1)}, bf16[64,1024]{1,0:T(8,128)(2,1)}, bf16[64,1024]{1,0:T(8,128)(2,1)}) custom-call(bf16[64,8192]{1,0:T(8,128)(2,1)S(1)} %get-tuple-element.8.refs_0_, bf16[64,8192]{1,0:T(8,128)(2,1)S(1)} %get-tuple-element.9.refs_1_, bf16[64,1024]{1,0:T(8,128)(2,1)S(1)} %get-tuple-element.10.refs_2_, ...), custom_call_target="tpu_custom_call" | custom-call | tf_op jit(solution)/shard_map/pallas_call | solution.py:406

commit v3 on v2

--- a/solution.py
+++ b/solution.py
@@ -17,6 +17,7 @@
 GROUP = 8
 WIDE = GROUP * DH
 PAIR = 2 * CHIP
+CHUNKS = GROUP // 2
 SCALE = DH ** (-0.5)
 MESH = pl.DeviceIdType.MESH
 F32 = jnp.float32
@@ -28,7 +29,7 @@
     q_in, k_in, v_in, g_in, len_in,
     att_out, dq_out, dk_out, dv_out,
     kv, qb, gb, ob, dqb, acc, gin, gout, fin, bias, lens,
-    key_pair, key_t, value_pair, value_t, scores, weights, probs, changes,
+    key_t, value_t, grad_t, scores, tops, rows, weights, probs, changes,
     k_own, v_own, q_away, g_away,
     len_sem, kv_recv, kv_fwd, own_ici, own_sib,
     qg_recv, qg_send, sum_recv, sum_send,
@@ -139,13 +140,14 @@
 
     def first_sum(h):
         for part in range(2):
-            gout[h, 0, part] = acc[h, part, 0:CHIP].astype(BF16)
+            gout[h, 0, part] = (acc[h, part, 0:CHIP] * (SCALE, 1.0)[part]).astype(BF16)
         sum_copy(h, 0).start()
 
     def next_sum(h, slot):
         pltpu.make_async_copy(gin.at[h, slot - 1], gin.at[h, slot - 1], sum_recv.at[h, slot - 1]).wait()
         for part in range(2):
-            total = gin[h, slot - 1, part].astype(F32) + acc[h, part, slot * CHIP:(slot + 1) * CHIP]
+            mine = acc[h, part, slot * CHIP:(slot + 1) * CHIP] * (SCALE, 1.0)[part]
+            total = gin[h, slot - 1, part].astype(F32) + mine
             if slot < 4:
                 gout[h, slot, part] = total.astype(BF16)
             else:
@@ -192,7 +194,7 @@
         copy.wait()
     pl.semaphore_wait(barrier, 5)
 
-    for h in range(3):
+    for h in range(2):
         own_ahead(h)
     for h in range(HEADS):
         start(own_to_sibling(h))
@@ -213,100 +215,120 @@
         bias[slot * CHIP:(slot + 1) * CHIP, :] = jnp.where(allowed, 0.0, -1e30)
 
     pass_on(0, 3)
+    own_ahead(2)
+    send_rows(1)
+    for h, slot in ((1, 3), (0, 2), (2, 3), (1, 2), (0, 1)):
+        pass_on(h, slot)
     own_ahead(3)
-    send_rows(1)
-    for h, slot in ((1, 3), (2, 3), (0, 2), (3, 3), (1, 2), (2, 2), (0, 1)):
-        pass_on(h, slot)
     send_rows(2)
-    for h, slot in ((3, 2), (1, 1), (2, 1)):
-        pass_on(h, slot)
+    pass_on(2, 2)
+    pass_on(1, 1)
     send_rows(3)
 
-    lane = lax.broadcasted_iota(jnp.int32, (PAIR, DH), 1)
-    key_lane = lax.broadcasted_iota(jnp.int32, (KEYS, DH), 1)
-    value_pair[:, DH:] = jnp.where(key_lane < 2, -1.0, 0.0).astype(BF16)
-    value_t[DH:, :] = jnp.ones((16, KEYS), BF16)
+    for side in range(2):
+        value_t[side, DH:, :] = jnp.ones((16, KEYS), BF16)
     blocks = [slice(slot * CHIP, (slot + 1) * CHIP) for slot in range(SLOTS)]
-    across = (((1,), (1,)), ((), ()))
+
+    def cols_of(c):
+        first = 2 * (c % CHUNKS)
+        return [slice((first + i) * DH, (first + i + 1) * DH) for i in range(2)]
 
     def prepare(h):
-        keys = kv[h, :, 0].reshape(KEYS, DH)
-        values = kv[h, :, 1].reshape(KEYS, DH)
-        key_t[...] = keys.T
-        value_t[:DH, :] = values.T
-        value_pair[:, :DH] = values
-        scaled = keys.astype(F32) * (SCALE * math.log2(math.e))
-        scaled_top = scaled.astype(BF16)
-        key_pair[:, :DH] = scaled_top
-        key_pair[:, DH:] = (scaled - scaled_top.astype(F32)).astype(BF16)
-
-    def chunk(h, p):
-        cols = [slice((2 * p + i) * DH, (2 * p + i + 1) * DH) for i in range(2)]
-        pair = slice(p * PAIR, (p + 1) * PAIR)
-        query = jnp.concatenate([qb[h, :, c] for c in cols], axis=0)
-        query = jnp.concatenate([query, query], axis=1)
+        key_t[h % 2] = kv[h, :, 0].reshape(KEYS, DH).T
+        value_t[h % 2, :DH, :] = kv[h, :, 1].reshape(KEYS, DH).T
+
+    def score_stage(c):
+        h, side = c // CHUNKS, c % 2
+        query = jnp.concatenate([qb[h, :, col].T for col in cols_of(c)], axis=1)
+        raw = jnp.dot(kv[h, :, 0].reshape(KEYS, DH), query, preferred_element_type=F32)
         top = None
         for block in blocks:
             one_bias = bias[block]
-            part = lax.dot_general(key_pair[block], query, across, preferred_element_type=F32)
-            part = part + jnp.concatenate([one_bias, one_bias], axis=1)
-            scores[block] = part
+            part = raw[block] * (SCALE * math.log2(math.e)) + jnp.concatenate([one_bias, one_bias], axis=1)
+            scores[side, block] = part
             part = jnp.max(part.reshape(CHIP // 8, 8, PAIR), axis=0)
             top = part if top is None else jnp.maximum(top, part)
-        top = jnp.max(top, axis=0, keepdims=True)
+        tops[side] = top
+
+    def out_stage(c):
+        h, side = c // CHUNKS, c % 2
+        top = jnp.max(tops[side], axis=0, keepdims=True)
         for block in blocks:
-            weights[block] = jnp.exp2(scores[block] - top).astype(BF16)
-        out = jnp.dot(value_t[...], weights[...], preferred_element_type=F32)
+            weights[side, block] = jnp.exp2(scores[side, block] - top).astype(BF16)
+        out = jnp.dot(value_t[h % 2], weights[side], preferred_element_type=F32)
         inverse = 1.0 / out[DH:DH + 1]
-        out = (out[:DH] * inverse).T.astype(BF16)
-        grad = jnp.concatenate([gb[h, :, c] for c in cols], axis=0)
-        for i, c in enumerate(cols):
-            ob[h, :, c] = out[i * CHIP:(i + 1) * CHIP]
-        delta = jnp.sum(out.astype(F32) * grad.astype(F32), axis=1, keepdims=True)
-        delta_top = delta.astype(BF16).astype(F32)
-        tail = jnp.where(lane == 0, delta_top, jnp.where(lane == 1, delta - delta_top, 0.0)).astype(BF16)
-        grad = jnp.concatenate([grad, tail], axis=1)
-        inverse = jnp.broadcast_to(inverse, (CHIP, PAIR)).astype(BF16)
+        out = out[:DH] * inverse
+        cols = cols_of(c)
+        grad = jnp.concatenate([gb[h, :, col].T for col in cols], axis=1)
+        grad_t[side] = grad
+        delta = jnp.sum(out.astype(BF16).astype(F32) * grad.astype(F32), axis=0, keepdims=True)
+        rows[side, 0] = jnp.broadcast_to(inverse, (8, PAIR))
+        rows[side, 1] = jnp.broadcast_to(delta, (8, PAIR))
+        out = out.T.astype(BF16)
+        for i, col in enumerate(cols):
+            ob[h, :, col] = out[i * CHIP:(i + 1) * CHIP]
+
+    def change_stage(c):
+        h, side = c // CHUNKS, c % 2
+        raw = jnp.dot(kv[h, :, 1].reshape(KEYS, DH), grad_t[side], preferred_element_type=F32)
+        inverse = jnp.broadcast_to(rows[side, 0, 0:1], (CHIP, PAIR)).astype(BF16)
+        delta = rows[side, 1, 0:1]
         for block in blocks:
-            change = lax.dot_general(value_pair[block], grad, across, preferred_element_type=F32).astype(BF16)
-            prob = weights[block] * inverse
-            probs[block, pair] = prob
-            changes[block, pair] = prob * change
-        query_grad = (jnp.dot(key_t[...], changes[:, pair], preferred_element_type=F32) * SCALE).T.astype(BF16)
-        for i, c in enumerate(cols):
-            dqb[h, :, c] = query_grad[i * CHIP:(i + 1) * CHIP]
-
-    def key_sums(h):
-        query = jnp.concatenate([qb[h, :, g * DH:(g + 1) * DH] for g in range(GROUP)], axis=0)
-        acc[h, 0] = jnp.dot(changes[...], query, preferred_element_type=F32) * SCALE
-        grad = jnp.concatenate([gb[h, :, g * DH:(g + 1) * DH] for g in range(GROUP)], axis=0)
-        acc[h, 1] = jnp.dot(probs[...], grad, preferred_element_type=F32)
+            prob = weights[side, block] * inverse
+            probs[side, block] = prob
+            changes[side, block] = prob * (raw[block] - delta).astype(BF16)
+
+    def grad_stage(c):
+        h, side = c // CHUNKS, c % 2
+        cols = cols_of(c)
+        query_grad = (jnp.dot(key_t[h % 2], changes[side], preferred_element_type=F32) * SCALE).T.astype(BF16)
+        for i, col in enumerate(cols):
+            dqb[h, :, col] = query_grad[i * CHIP:(i + 1) * CHIP]
+        for part, (left, right) in enumerate(((changes, qb), (probs, gb))):
+            right = jnp.concatenate([right[h, :, col] for col in cols], axis=0)
+            total = jnp.dot(left[side], right, preferred_element_type=F32)
+            if c % CHUNKS == 0:
+                acc[h, part] = total
+            else:
+                acc[h, part] += total
 
     after = {
-        (0, 0): [(pass_on, 3, 1)],
-        (1, 2): [(next_sum, 0, 1)],
-        (2, 1): [(next_sum, 0, 2)],
-        (2, 2): [(next_sum, 1, 1)],
-        (3, 0): [(next_sum, 0, 3)],
-        (3, 1): [(next_sum, 1, 2)],
-        (3, 2): [(next_sum, 2, 1)],
-        (3, 3): [(next_sum, 0, 4), (next_sum, 1, 3)],
+        0: [(pass_on, 3, 3)],
+        1: [(pass_on, 2, 1)],
+        3: [(pass_on, 3, 2)],
+        6: [(pass_on, 3, 1)],
+        9: [(next_sum, 0, 1)],
+        12: [(next_sum, 0, 2)],
+        13: [(next_sum, 1, 1)],
+        15: [(next_sum, 0, 3)],
+        16: [(next_sum, 1, 2)],
+        17: [(next_sum, 2, 1)],
+        18: [(next_sum, 0, 4)],
     }
-    for h in range(HEADS):
-        wait_rows(h)
-        wait_kv(h, 4)
-        wait_kv(h, 0)
-        prepare(h)
-        for p in range(GROUP // 2):
-            chunk(h, p)
-            if p == GROUP // 2 - 1:
-                key_sums(h)
+    steps = HEADS * CHUNKS
+    for step in range(steps + 3):
+        if step < steps and step % CHUNKS == 0:
+            h = step // CHUNKS
+            wait_rows(h)
+            wait_kv(h, 4)
+            wait_kv(h, 0)
+            prepare(h)
+        if step < steps:
+            score_stage(step)
+        if 0 <= step - 2 < steps:
+            change_stage(step - 2)
+        if 0 <= step - 1 < steps:
+            out_stage(step - 1)
+        if 0 <= step - 3:
+            grad_stage(step - 3)
+            if (step - 3) % CHUNKS == CHUNKS - 1:
+                h = (step - 3) // CHUNKS
                 first_sum(h)
                 start(out_remote(h))
                 keep_out(h)
-            for event, *where in after.get((h, p), []):
-                event(*where)
-    for h, slot in ((2, 2), (3, 1), (1, 4), (2, 3), (3, 2), (2, 4), (3, 3), (3, 4)):
+        for event, *where in after.get(step, []):
+            event(*where)
+    for h, slot in ((1, 3), (2, 2), (3, 1), (1, 4), (2, 3), (3, 2), (2, 4), (3, 3), (3, 4)):
         next_sum(h, slot)
 
     for h in range(HEADS):
@@ -366,14 +388,15 @@
                 pltpu.VMEM((HEADS, 2, CHIP, DH), BF16),
                 pltpu.VMEM((KEYS, DH), F32),
                 pltpu.VMEM((1, 128), jnp.int32),
-                pltpu.VMEM((KEYS, 2 * DH), BF16),
-                pltpu.VMEM((DH, KEYS), BF16),
-                pltpu.VMEM((KEYS, 2 * DH), BF16),
-                pltpu.VMEM((DH + 16, KEYS), BF16),
-                pltpu.VMEM((KEYS, PAIR), F32),
-                pltpu.VMEM((KEYS, PAIR), BF16),
-                pltpu.VMEM((KEYS, GROUP * CHIP), BF16),
-                pltpu.VMEM((KEYS, GROUP * CHIP), BF16),
+                pltpu.VMEM((2, DH, KEYS), BF16),
+                pltpu.VMEM((2, DH + 16, KEYS), BF16),
+                pltpu.VMEM((2, DH, PAIR), BF16),
+                pltpu.VMEM((2, KEYS, PAIR), F32),
+                pltpu.VMEM((2, 8, PAIR), F32),
+                pltpu.VMEM((2, 2, 8, PAIR), F32),
+                pltpu.VMEM((2, KEYS, PAIR), BF16),
+                pltpu.VMEM((2, KEYS, PAIR), BF16),
+                pltpu.VMEM((2, KEYS, PAIR), BF16),
                 pltpu.VMEM((ROWS, 2 * HEADS * DH), BF16),
                 pltpu.VMEM((ROWS, 2 * HEADS * DH), BF16),
                 pltpu.VMEM((HEADS, ROWS, WIDE), BF16),

time: 78.4 us -> 74 us (0.944)
  Pallas kernels: 77.5 us -> 73.2 us
    pallas_call x1, Pallas kernels: 76 us -> 71.7 us  [per_device(): pl.pallas_call(functools.partial(kernel, devices), out_shape=tuple((pltpu...]
where the time goes in v3:
time: 74 us; the launch traced here: 73.8 us
  Pallas kernels  73.2 us (99%)
    pallas_call x1, Pallas kernels, per_device(): pl.pallas_call(functools.partial(kernel, devices), out_shape=tuple((pltpu...  71.7 us

profile of v3, /device:TPU:1, one launch (start us, length us, event | category | flops | bytes accessed | tf_op | source)
XLA Modules:
  0.0 73.8 jit_solution(16074469338867059332)
XLA Ops:
  0.6 71.7 %shard_map.84 = (bf16[64,8192]{1,0:T(8,128)(2,1)S(1)}, bf16[64,8192]{1,0:T(8,128)(2,1)S(1)}, bf16[64,1024]{1,0:T(8,128)(2,1)S(1)}, bf16[64,1024]{1,0:T(8,128)(2,1)S(1)}) custom-call(bf16[64,8192]{1,0:T(8,128)(2,1)} %q_in.1, bf16[64,1024]{1,0:T(8,128)(2,1)} %k_in.1, bf16[64,1024]{1,0:T(8,128)(2,1)} %v_in.1, bf16[64,8192]{1,0:T(8,128)(2,1)} %g_in.1, ...), custom_call_target="tpu_custom_call" | custom-call | flops 4026531840 | bytes 5242880 | tf_op jit(solution)/shard_map/pallas_call | solution.py:374
  72.3 1.5 %shard_map.85 = (bf16[64,8192]{1,0:T(8,128)(2,1)}, bf16[64,8192]{1,0:T(8,128)(2,1)}, bf16[64,1024]{1,0:T(8,128)(2,1)}, bf16[64,1024]{1,0:T(8,128)(2,1)}) custom-call(bf16[64,8192]{1,0:T(8,128)(2,1)S(1)} %get-tuple-element.8.refs_0_, bf16[64,8192]{1,0:T(8,128)(2,1)S(1)} %get-tuple-element.9.refs_1_, bf16[64,1024]{1,0:T(8,128)(2,1)S(1)} %get-tuple-element.10.refs_2_, ...), custom_call_target="tpu_custom_call" | custom-call | tf_op jit(solution)/shard_map/pallas_call | solution.py:429

commit v4 on v3

--- a/solution.py
+++ b/solution.py
@@ -68,20 +68,20 @@
             for part, src in enumerate((k_own, v_own)):
                 made.append(remote(
                     src.at[:, head_cols(owner, h, DH)], kv.at[h, 3, part, my_rows],
-                    own_ici.at[h, side, part], kv_recv.at[h, 3], target,
+                    own_ici.at[h, side, part], kv_recv.at[h, 3, part], target,
                 ))
         return made
 
     def own_to_sibling(h):
         return [
             remote(src.at[:, head_cols(other, h, DH)], kv.at[h, 4, part, my_rows],
-                   own_sib.at[h, part], kv_recv.at[h, 4], sibling)
+                   own_sib.at[h, part], kv_recv.at[h, 4, part], sibling)
             for part, src in enumerate((k_own, v_own))
         ]
 
     def own_local(h):
         return [
-            pltpu.make_async_copy(src.at[:, head_cols(core, h, DH)], kv.at[h, 4, part, my_rows], kv_recv.at[h, 4])
+            pltpu.make_async_copy(src.at[:, head_cols(core, h, DH)], kv.at[h, 4, part, my_rows], kv_recv.at[h, 4, part])
             for part, src in enumerate((k_in, v_in))
         ]
 
@@ -118,56 +118,57 @@
         for copy in copies:
             copy.start()
 
-    def wait_kv(h, slot):
-        pltpu.make_async_copy(kv.at[h, slot], kv.at[h, slot], kv_recv.at[h, slot]).wait()
+    def wait_kv(h, slot, part):
+        ref = kv.at[h, slot, part]
+        pltpu.make_async_copy(ref, ref, kv_recv.at[h, slot, part]).wait()
 
     def wait_rows(h):
         for part, dst in enumerate((qb, gb)):
             pltpu.make_async_copy(dst.at[h], dst.at[h], qg_recv.at[h, part]).wait()
 
-    def forward(h, slot):
-        return remote(kv.at[h, slot], kv.at[h, slot - 1], kv_fwd.at[h, slot - 1], kv_recv.at[h, slot - 1], ahead)
+    def forward(h, slot, part):
+        return remote(kv.at[h, slot, part], kv.at[h, slot - 1, part],
+                      kv_fwd.at[h, slot - 1, part], kv_recv.at[h, slot - 1, part], ahead)
 
     def own_ahead(h):
         start(own_to_ahead(h))
 
     def pass_on(h, slot):
-        wait_kv(h, slot)
-        forward(h, slot).start()
-
-    def sum_copy(h, slot):
-        return remote(gout.at[h, slot], gin.at[h, slot], sum_send.at[h, slot], sum_recv.at[h, slot], behind)
+        for part in range(2):
+            wait_kv(h, slot, part)
+            forward(h, slot, part).start()
+
+    def sum_copy(h, slot, part):
+        return remote(gout.at[h, slot, part], gin.at[h, slot, part],
+                      sum_send.at[h, slot, part], sum_recv.at[h, slot, part], behind)
 
     def first_sum(h):
         for part in range(2):
             gout[h, 0, part] = (acc[h, part, 0:CHIP] * (SCALE, 1.0)[part]).astype(BF16)
-        sum_copy(h, 0).start()
+            sum_copy(h, 0, part).start()
 
     def next_sum(h, slot):
-        pltpu.make_async_copy(gin.at[h, slot - 1], gin.at[h, slot - 1], sum_recv.at[h, slot - 1]).wait()
         for part in range(2):
+            ref = gin.at[h, slot - 1, part]
+            pltpu.make_async_copy(ref, ref, sum_recv.at[h, slot - 1, part]).wait()
             mine = acc[h, part, slot * CHIP:(slot + 1) * CHIP] * (SCALE, 1.0)[part]
             total = gin[h, slot - 1, part].astype(F32) + mine
             if slot < 4:
                 gout[h, slot, part] = total.astype(BF16)
+                sum_copy(h, slot, part).start()
             else:
                 fin[h, part] = total.astype(BF16)
-        if slot < 4:
-            sum_copy(h, slot).start()
-        else:
-            start(fin_remote(h))
+                fin_remote(h, part).start()
+        if slot == 4:
             keep_fin(h)
 
     def keep_fin(h):
         for part, dst in enumerate((dk_out, dv_out)):
             dst[:, head_cols(core, h, DH)] = fin[h, part, my_rows]
 
-    def fin_remote(h):
-        return [
-            remote(fin.at[h, part, sib_rows], dst.at[:, head_cols(core, h, DH)],
-                   fin_send.at[h, part], fin_recv.at[h, part], sibling)
-            for part, dst in enumerate((dk_out, dv_out))
-        ]
+    def fin_remote(h, part):
+        return remote(fin.at[h, part, sib_rows], (dk_out, dv_out)[part].at[:, head_cols(core, h, DH)],
+                      fin_send.at[h, part], fin_recv.at[h, part], sibling)
 
     def keep_out(h):
         for src, dst in ((ob, att_out), (dqb, dq_out)):
@@ -194,11 +195,11 @@
         copy.wait()
     pl.semaphore_wait(barrier, 5)
 
-    for h in range(2):
-        own_ahead(h)
-    for h in range(HEADS):
+    own_ahead(0)
+    start(own_to_sibling(0))
+    send_rows(0)
+    for h in range(1, HEADS):
         start(own_to_sibling(h))
-    send_rows(0)
 
     len_copy.wait()
     first_pos = (chip_base // 2) * CHIP
@@ -215,15 +216,11 @@
         bias[slot * CHIP:(slot + 1) * CHIP, :] = jnp.where(allowed, 0.0, -1e30)
 
     pass_on(0, 3)
-    own_ahead(2)
+    pass_on(0, 2)
+    own_ahead(1)
+    pass_on(0, 1)
     send_rows(1)
-    for h, slot in ((1, 3), (0, 2), (2, 3), (1, 2), (0, 1)):
-        pass_on(h, slot)
-    own_ahead(3)
-    send_rows(2)
-    pass_on(2, 2)
-    pass_on(1, 1)
-    send_rows(3)
+    pass_on(1, 3)
 
     for side in range(2):
         value_t[side, DH:, :] = jnp.ones((16, KEYS), BF16)
@@ -232,10 +229,6 @@
     def cols_of(c):
         first = 2 * (c % CHUNKS)
         return [slice((first + i) * DH, (first + i + 1) * DH) for i in range(2)]
-
-    def prepare(h):
-        key_t[h % 2] = kv[h, :, 0].reshape(KEYS, DH).T
-        value_t[h % 2, :DH, :] = kv[h, :, 1].reshape(KEYS, DH).T
 
     def score_stage(c):
         h, side = c // CHUNKS, c % 2
@@ -292,53 +285,62 @@
             else:
                 acc[h, part] += total
 
-    after = {
-        0: [(pass_on, 3, 3)],
-        1: [(pass_on, 2, 1)],
-        3: [(pass_on, 3, 2)],
-        6: [(pass_on, 3, 1)],
-        9: [(next_sum, 0, 1)],
-        12: [(next_sum, 0, 2)],
-        13: [(next_sum, 1, 1)],
-        15: [(next_sum, 0, 3)],
-        16: [(next_sum, 1, 2)],
-        17: [(next_sum, 2, 1)],
-        18: [(next_sum, 0, 4)],
-    }
-    steps = HEADS * CHUNKS
-    for step in range(steps + 3):
-        if step < steps and step % CHUNKS == 0:
-            h = step // CHUNKS
-            wait_rows(h)
-            wait_kv(h, 4)
-            wait_kv(h, 0)
-            prepare(h)
-        if step < steps:
-            score_stage(step)
-        if 0 <= step - 2 < steps:
-            change_stage(step - 2)
-        if 0 <= step - 1 < steps:
-            out_stage(step - 1)
-        if 0 <= step - 3:
-            grad_stage(step - 3)
-            if (step - 3) % CHUNKS == CHUNKS - 1:
-                h = (step - 3) // CHUNKS
-                first_sum(h)
-                start(out_remote(h))
-                keep_out(h)
-        for event, *where in after.get(step, []):
-            event(*where)
-    for h, slot in ((1, 3), (2, 2), (3, 1), (1, 4), (2, 3), (3, 2), (2, 4), (3, 3), (3, 4)):
+    def events(h, step):
+        if step == 0:
+            if h + 1 < HEADS:
+                pass_on(h + 1, 2)
+            if h + 2 < HEADS:
+                own_ahead(h + 2)
+                send_rows(h + 2)
+        if step == 1 and h >= 2:
+            next_sum(h - 2, 4)
+        if step == 2 and h >= 1:
+            next_sum(h - 1, 1)
+        if step == 4:
+            if h + 1 < HEADS:
+                pass_on(h + 1, 1)
+            if h + 2 < HEADS:
+                pass_on(h + 2, 3)
+            if h >= 1:
+                next_sum(h - 1, 2)
+
+    for h in range(HEADS):
+        wait_rows(h)
+        for slot in (4, 0):
+            wait_kv(h, slot, 0)
+        key_t[h % 2] = kv[h, :, 0].reshape(KEYS, DH).T
+        for step in range(CHUNKS + 3):
+            c = h * CHUNKS + step
+            if step < CHUNKS:
+                score_stage(c)
+            if step == 0:
+                for slot in (4, 0):
+                    wait_kv(h, slot, 1)
+                value_t[h % 2, :DH, :] = kv[h, :, 1].reshape(KEYS, DH).T
+            if 0 <= step - 2 < CHUNKS:
+                change_stage(c - 2)
+            if 0 <= step - 1 < CHUNKS:
+                out_stage(c - 1)
+            if 0 <= step - 3:
+                grad_stage(c - 3)
+            events(h, step)
+        first_sum(h)
+        start(out_remote(h))
+        keep_out(h)
+        if h >= 1:
+            next_sum(h - 1, 3)
+    for h, slot in ((3, 1), (2, 4), (3, 2), (3, 3), (3, 4)):
         next_sum(h, slot)
 
     for h in range(HEADS):
         for copy in own_to_ahead(h) + own_to_sibling(h) + rows_to_sibling(h):
             copy.wait_send()
-        for slot in (3, 2, 1):
-            forward(h, slot).wait_send()
-        for slot in range(4):
-            sum_copy(h, slot).wait_send()
-        for copy in out_remote(h) + fin_remote(h):
+        for part in range(2):
+            for slot in (3, 2, 1):
+                forward(h, slot, part).wait_send()
+            for slot in range(4):
+                sum_copy(h, slot, part).wait_send()
+        for copy in out_remote(h) + [fin_remote(h, part) for part in range(2)]:
             copy.wait_send()
         for part, dst in enumerate((att_out, dq_out)):
             ref = dst.at[:, head_cols(other, h, WIDE)]
@@ -402,14 +404,14 @@
                 pltpu.VMEM((HEADS, ROWS, WIDE), BF16),
                 pltpu.VMEM((HEADS, ROWS, WIDE), BF16),
                 dma,
-                dma((HEADS, SLOTS)),
-                dma((HEADS, 3)),
+                dma((HEADS, SLOTS, 2)),
+                dma((HEADS, 3, 2)),
                 dma((HEADS, 2, 2)),
                 dma((HEADS, 2)),
                 dma((HEADS, 2)),
                 dma((HEADS, 2)),
-                dma((HEADS, 4)),
-                dma((HEADS, 4)),
+                dma((HEADS, 4, 2)),
+                dma((HEADS, 4, 2)),
                 dma((HEADS, 2)),
                 dma((HEADS, 2)),
                 dma((HEADS, 2)),

time: 74 us -> 81.5 us (1.10)
  Pallas kernels: 73.2 us -> 80.7 us
    pallas_call x1, Pallas kernels: 71.7 us -> 79.2 us  [per_device(): pl.pallas_call(functools.partial(kernel, devices), out_shape=tuple((pltpu...]
where the time goes in v4:
time: 81.5 us; the launch traced here: 81.4 us
  Pallas kernels  80.7 us (99%)
    pallas_call x1, Pallas kernels, per_device(): pl.pallas_call(functools.partial(kernel, devices), out_shape=tuple((pltpu...  79.2 us

profile of v4, /device:TPU:1, one launch (start us, length us, event | category | flops | bytes accessed | tf_op | source)
XLA Modules:
  0.0 81.4 jit_solution(15572568423034439714)
XLA Ops:
  0.6 79.2 %shard_map.84 = (bf16[64,8192]{1,0:T(8,128)(2,1)S(1)}, bf16[64,8192]{1,0:T(8,128)(2,1)S(1)}, bf16[64,1024]{1,0:T(8,128)(2,1)S(1)}, bf16[64,1024]{1,0:T(8,128)(2,1)S(1)}) custom-call(bf16[64,8192]{1,0:T(8,128)(2,1)} %q_in.1, bf16[64,1024]{1,0:T(8,128)(2,1)} %k_in.1, bf16[64,1024]{1,0:T(8,128)(2,1)} %v_in.1, bf16[64,8192]{1,0:T(8,128)(2,1)} %g_in.1, ...), custom_call_target="tpu_custom_call" | custom-call | flops 4026531840 | bytes 5242880 | tf_op jit(solution)/shard_map/pallas_call | solution.py:376
  79.9 1.5 %shard_map.85 = (bf16[64,8192]{1,0:T(8,128)(2,1)}, bf16[64,8192]{1,0:T(8,128)(2,1)}, bf16[64,1024]{1,0:T(8,128)(2,1)}, bf16[64,1024]{1,0:T(8,128)(2,1)}) custom-call(bf16[64,8192]{1,0:T(8,128)(2,1)S(1)} %get-tuple-element.8.refs_0_, bf16[64,8192]{1,0:T(8,128)(2,1)S(1)} %get-tuple-element.9.refs_1_, bf16[64,1024]{1,0:T(8,128)(2,1)S(1)} %get-tuple-element.10.refs_2_, ...), custom_call_target="tpu_custom_call" | custom-call | tf_op jit(solution)/shard_map/pallas_call | solution.py:431

commit v5 on v4

--- a/solution.py
+++ b/solution.py
@@ -170,16 +170,13 @@
         return remote(fin.at[h, part, sib_rows], (dk_out, dv_out)[part].at[:, head_cols(core, h, DH)],
                       fin_send.at[h, part], fin_recv.at[h, part], sibling)
 
-    def keep_out(h):
-        for src, dst in ((ob, att_out), (dqb, dq_out)):
-            dst[:, head_cols(core, h, WIDE)] = src[h, my_rows]
-
-    def out_remote(h):
-        return [
-            remote(src.at[h, sib_rows], dst.at[:, head_cols(core, h, WIDE)],
-                   out_send.at[h, part], out_recv.at[h, part], sibling)
-            for part, (src, dst) in enumerate(((ob, att_out), (dqb, dq_out)))
-        ]
+    def out_remote(h, part):
+        return remote((ob, dqb)[part].at[h, sib_rows], (att_out, dq_out)[part].at[:, head_cols(core, h, WIDE)],
+                      out_send.at[h, part], out_recv.at[h, part], sibling)
+
+    def give_out(h, part):
+        out_remote(h, part).start()
+        (att_out, dq_out)[part][:, head_cols(core, h, WIDE)] = (ob, dqb)[part][h, my_rows]
 
     barrier = pltpu.get_barrier_semaphore()
     for peer in (sibling, ahead, ahead_other, behind, behind_other):
@@ -195,11 +192,11 @@
         copy.wait()
     pl.semaphore_wait(barrier, 5)
 
-    own_ahead(0)
-    start(own_to_sibling(0))
+    for h in range(2):
+        own_ahead(h)
+    for h in range(HEADS):
+        start(own_to_sibling(h))
     send_rows(0)
-    for h in range(1, HEADS):
-        start(own_to_sibling(h))
 
     len_copy.wait()
     first_pos = (chip_base // 2) * CHIP
@@ -216,11 +213,17 @@
         bias[slot * CHIP:(slot + 1) * CHIP, :] = jnp.where(allowed, 0.0, -1e30)
 
     pass_on(0, 3)
-    pass_on(0, 2)
-    own_ahead(1)
-    pass_on(0, 1)
     send_rows(1)
     pass_on(1, 3)
+    pass_on(0, 2)
+    own_ahead(2)
+    pass_on(1, 2)
+    pass_on(0, 1)
+    own_ahead(3)
+    send_rows(2)
+    pass_on(2, 3)
+    pass_on(1, 1)
+    send_rows(3)
 
     for side in range(2):
         value_t[side, DH:, :] = jnp.ones((16, KEYS), BF16)
@@ -229,6 +232,10 @@
     def cols_of(c):
         first = 2 * (c % CHUNKS)
         return [slice((first + i) * DH, (first + i + 1) * DH) for i in range(2)]
+
+    def prepare(h):
+        key_t[h] = kv[h, :, 0].reshape(KEYS, DH).T
+        value_t[h % 2, :DH, :] = kv[h, :, 1].reshape(KEYS, DH).T
 
     def score_stage(c):
         h, side = c // CHUNKS, c % 2
@@ -269,67 +276,64 @@
         for block in blocks:
             prob = weights[side, block] * inverse
             probs[side, block] = prob
-            changes[side, block] = prob * (raw[block] - delta).astype(BF16)
-
-    def grad_stage(c):
-        h, side = c // CHUNKS, c % 2
-        cols = cols_of(c)
-        query_grad = (jnp.dot(key_t[h % 2], changes[side], preferred_element_type=F32) * SCALE).T.astype(BF16)
-        for i, col in enumerate(cols):
-            dqb[h, :, col] = query_grad[i * CHIP:(i + 1) * CHIP]
-        for part, (left, right) in enumerate(((changes, qb), (probs, gb))):
-            right = jnp.concatenate([right[h, :, col] for col in cols], axis=0)
-            total = jnp.dot(left[side], right, preferred_element_type=F32)
+            changes[c, block] = prob * (raw[block] - delta).astype(BF16)
+
+    def key_stage(c):
+        h = c // CHUNKS
+        for part, (left, right) in enumerate(((changes.at[c], qb), (probs.at[c % 2], gb))):
+            right = jnp.concatenate([right[h, :, col] for col in cols_of(c)], axis=0)
+            total = jnp.dot(left[...], right, preferred_element_type=F32)
             if c % CHUNKS == 0:
                 acc[h, part] = total
             else:
                 acc[h, part] += total
 
-    def events(h, step):
-        if step == 0:
-            if h + 1 < HEADS:
-                pass_on(h + 1, 2)
-            if h + 2 < HEADS:
-                own_ahead(h + 2)
-                send_rows(h + 2)
-        if step == 1 and h >= 2:
-            next_sum(h - 2, 4)
-        if step == 2 and h >= 1:
-            next_sum(h - 1, 1)
-        if step == 4:
-            if h + 1 < HEADS:
-                pass_on(h + 1, 1)
-            if h + 2 < HEADS:
-                pass_on(h + 2, 3)
-            if h >= 1:
-                next_sum(h - 1, 2)
-
-    for h in range(HEADS):
-        wait_rows(h)
-        for slot in (4, 0):
-            wait_kv(h, slot, 0)
-        key_t[h % 2] = kv[h, :, 0].reshape(KEYS, DH).T
-        for step in range(CHUNKS + 3):
-            c = h * CHUNKS + step
-            if step < CHUNKS:
-                score_stage(c)
-            if step == 0:
-                for slot in (4, 0):
-                    wait_kv(h, slot, 1)
-                value_t[h % 2, :DH, :] = kv[h, :, 1].reshape(KEYS, DH).T
-            if 0 <= step - 2 < CHUNKS:
-                change_stage(c - 2)
-            if 0 <= step - 1 < CHUNKS:
-                out_stage(c - 1)
-            if 0 <= step - 3:
-                grad_stage(c - 3)
-            events(h, step)
-        first_sum(h)
-        start(out_remote(h))
-        keep_out(h)
-        if h >= 1:
-            next_sum(h - 1, 3)
-    for h, slot in ((3, 1), (2, 4), (3, 2), (3, 3), (3, 4)):
+    def query_stage(h):
+        for c in range(h * CHUNKS, (h + 1) * CHUNKS):
+            query_grad = (jnp.dot(key_t[h], changes[c], preferred_element_type=F32) * SCALE).T.astype(BF16)
+            for i, col in enumerate(cols_of(c)):
+                dqb[h, :, col] = query_grad[i * CHIP:(i + 1) * CHIP]
+        give_out(h, 1)
+
+    after = {
+        1: [(pass_on, 2, 2), (pass_on, 3, 3)],
+        5: [(pass_on, 2, 1), (pass_on, 3, 2)],
+        9: [(pass_on, 3, 1)],
+        10: [(next_sum, 0, 1)],
+        14: [(next_sum, 0, 2), (next_sum, 1, 1)],
+    }
+    steps = HEADS * CHUNKS
+    for step in range(steps + 3):
+        if step < steps and step % CHUNKS == 0:
+            h = step // CHUNKS
+            wait_rows(h)
+            for slot in (4, 0):
+                for part in range(2):
+                    wait_kv(h, slot, part)
+            prepare(h)
+        if step < steps:
+            score_stage(step)
+        if 0 <= step - 2 < steps:
+            change_stage(step - 2)
+        if 0 <= step - 1 < steps:
+            out_stage(step - 1)
+        if 0 <= step - 3:
+            key_stage(step - 3)
+            if (step - 3) % CHUNKS == CHUNKS - 1:
+                h = (step - 3) // CHUNKS
+                first_sum(h)
+                give_out(h, 0)
+        for event, *where in after.get(step, []):
+            event(*where)
+    for h, slot in ((0, 3), (1, 2), (2, 1)):
+        next_sum(h, slot)
+    query_stage(0)
+    query_stage(1)
+    for h, slot in ((0, 4), (1, 3), (2, 2), (3, 1)):
+        next_sum(h, slot)
+    query_stage(2)
+    query_stage(3)
+    for h, slot in ((1, 4), (2, 3), (3, 2), (2, 4), (3, 3), (3, 4)):
         next_sum(h, slot)
 
     for h in range(HEADS):
@@ -340,8 +344,8 @@
                 forward(h, slot, part).wait_send()
             for slot in range(4):
                 sum_copy(h, slot, part).wait_send()
-        for copy in out_remote(h) + [fin_remote(h, part) for part in range(2)]:
-            copy.wait_send()
+            out_remote(h, part).wait_send()
+            fin_remote(h, part).wait_send()
         for part, dst in enumerate((att_out, dq_out)):
             ref = dst.at[:, head_cols(other, h, WIDE)]
             pltpu.make_async_copy(ref, ref, out_recv.at[h, part]).wait()
@@ -390,7 +394,7 @@
                 pltpu.VMEM((HEADS, 2, CHIP, DH), BF16),
                 pltpu.VMEM((KEYS, DH), F32),
                 pltpu.VMEM((1, 128), jnp.int32),
-                pltpu.VMEM((2, DH, KEYS), BF16),
+                pltpu.VMEM((HEADS, DH, KEYS), BF16),
                 pltpu.VMEM((2, DH + 16, KEYS), BF16),
                 pltpu.VMEM((2, DH, PAIR), BF16),
                 pltpu.VMEM((2, KEYS, PAIR), F32),
@@ -398,7 +402,7 @@
                 pltpu.VMEM((2, 2, 8, PAIR), F32),
                 pltpu.VMEM((2, KEYS, PAIR), BF16),
                 pltpu.VMEM((2, KEYS, PAIR), BF16),
-                pltpu.VMEM((2, KEYS, PAIR), BF16),
+                pltpu.VMEM((HEADS * CHUNKS, KEYS, PAIR), BF16),
                 pltpu.VMEM((ROWS, 2 * HEADS * DH), BF16),
                 pltpu.VMEM((ROWS, 2 * HEADS * DH), BF16),
                 pltpu.VMEM((HEADS, ROWS, WIDE), BF16),

time: 81.5 us -> 74.4 us (0.913)
  Pallas kernels: 80.7 us -> 73.6 us
    pallas_call x1, Pallas kernels: 79.2 us -> 72.1 us  [per_device(): pl.pallas_call(functools.partial(kernel, devices), out_shape=tuple((pltpu...]
where the time goes in v5:
time: 74.4 us; the launch traced here: 74.2 us
  Pallas kernels  73.6 us (99%)
    pallas_call x1, Pallas kernels, per_device(): pl.pallas_call(functools.partial(kernel, devices), out_shape=tuple((pltpu...  72.1 us

profile of v5, /device:TPU:1, one launch (start us, length us, event | category | flops | bytes accessed | tf_op | source)
XLA Modules:
  0.0 74.2 jit_solution(2935810155160325164)
XLA Ops:
  0.6 72.1 %shard_map.84 = (bf16[64,8192]{1,0:T(8,128)(2,1)S(1)}, bf16[64,8192]{1,0:T(8,128)(2,1)S(1)}, bf16[64,1024]{1,0:T(8,128)(2,1)S(1)}, bf16[64,1024]{1,0:T(8,128)(2,1)S(1)}) custom-call(bf16[64,8192]{1,0:T(8,128)(2,1)} %q_in.1, bf16[64,1024]{1,0:T(8,128)(2,1)} %k_in.1, bf16[64,1024]{1,0:T(8,128)(2,1)} %v_in.1, bf16[64,8192]{1,0:T(8,128)(2,1)} %g_in.1, ...), custom_call_target="tpu_custom_call" | custom-call | flops 4026531840 | bytes 5242880 | tf_op jit(solution)/shard_map/pallas_call | solution.py:380
  72.7 1.5 %shard_map.85 = (bf16[64,8192]{1,0:T(8,128)(2,1)}, bf16[64,8192]{1,0:T(8,128)(2,1)}, bf16[64,1024]{1,0:T(8,128)(2,1)}, bf16[64,1024]{1,0:T(8,128)(2,1)}) custom-call(bf16[64,8192]{1,0:T(8,128)(2,1)S(1)} %get-tuple-element.8.refs_0_, bf16[64,8192]{1,0:T(8,128)(2,1)S(1)} %get-tuple-element.9.refs_1_, bf16[64,1024]{1,0:T(8,128)(2,1)S(1)} %get-tuple-element.10.refs_2_, ...), custom_call_target="tpu_custom_call" | custom-call | tf_op jit(solution)/shard_map/pallas_call | solution.py:435

commit v6 on v5

--- a/solution.py
+++ b/solution.py
@@ -29,7 +29,7 @@
     q_in, k_in, v_in, g_in, len_in,
     att_out, dq_out, dk_out, dv_out,
     kv, qb, gb, ob, dqb, acc, gin, gout, fin, bias, lens,
-    key_t, value_t, grad_t, scores, tops, rows, weights, probs, changes,
+    value_t, grad_t, scores, tops, rows, probs, changes,
     k_own, v_own, q_away, g_away,
     len_sem, kv_recv, kv_fwd, own_ici, own_sib,
     qg_recv, qg_send, sum_recv, sum_send,
@@ -133,8 +133,8 @@
     def own_ahead(h):
         start(own_to_ahead(h))
 
-    def pass_on(h, slot):
-        for part in range(2):
+    def pass_on(h, slot, parts=(0, 1)):
+        for part in parts:
             wait_kv(h, slot, part)
             forward(h, slot, part).start()
 
@@ -142,29 +142,25 @@
         return remote(gout.at[h, slot, part], gin.at[h, slot, part],
                       sum_send.at[h, slot, part], sum_recv.at[h, slot, part], behind)
 
-    def first_sum(h):
-        for part in range(2):
-            gout[h, 0, part] = (acc[h, part, 0:CHIP] * (SCALE, 1.0)[part]).astype(BF16)
-            sum_copy(h, 0, part).start()
-
-    def next_sum(h, slot):
-        for part in range(2):
-            ref = gin.at[h, slot - 1, part]
-            pltpu.make_async_copy(ref, ref, sum_recv.at[h, slot - 1, part]).wait()
-            mine = acc[h, part, slot * CHIP:(slot + 1) * CHIP] * (SCALE, 1.0)[part]
-            total = gin[h, slot - 1, part].astype(F32) + mine
-            if slot < 4:
-                gout[h, slot, part] = total.astype(BF16)
-                sum_copy(h, slot, part).start()
-            else:
-                fin[h, part] = total.astype(BF16)
-                fin_remote(h, part).start()
-        if slot == 4:
-            keep_fin(h)
-
-    def keep_fin(h):
-        for part, dst in enumerate((dk_out, dv_out)):
-            dst[:, head_cols(core, h, DH)] = fin[h, part, my_rows]
+    def first_sum(h, part):
+        gout[h, 0, part] = (acc[h, part, 0:CHIP] * (SCALE, 1.0)[part]).astype(BF16)
+        sum_copy(h, 0, part).start()
+
+    def next_sum(h, part, slot):
+        ref = gin.at[h, slot - 1, part]
+        pltpu.make_async_copy(ref, ref, sum_recv.at[h, slot - 1, part]).wait()
+        mine = acc[h, part, slot * CHIP:(slot + 1) * CHIP] * (SCALE, 1.0)[part]
+        total = gin[h, slot - 1, part].astype(F32) + mine
+        if slot < 4:
+            gout[h, slot, part] = total.astype(BF16)
+            sum_copy(h, slot, part).start()
+        else:
+            fin[h, part] = total.astype(BF16)
+            fin_remote(h, part).start()
+            keep_fin(h, part)
+
+    def keep_fin(h, part):
+        (dk_out, dv_out)[part][:, head_cols(core, h, DH)] = fin[h, part, my_rows]
 
     def fin_remote(h, part):
         return remote(fin.at[h, part, sib_rows], (dk_out, dv_out)[part].at[:, head_cols(core, h, DH)],
@@ -225,17 +221,11 @@
     pass_on(1, 1)
     send_rows(3)
 
-    for side in range(2):
-        value_t[side, DH:, :] = jnp.ones((16, KEYS), BF16)
     blocks = [slice(slot * CHIP, (slot + 1) * CHIP) for slot in range(SLOTS)]
 
     def cols_of(c):
         first = 2 * (c % CHUNKS)
         return [slice((first + i) * DH, (first + i + 1) * DH) for i in range(2)]
-
-    def prepare(h):
-        key_t[h] = kv[h, :, 0].reshape(KEYS, DH).T
-        value_t[h % 2, :DH, :] = kv[h, :, 1].reshape(KEYS, DH).T
 
     def score_stage(c):
         h, side = c // CHUNKS, c % 2
@@ -250,20 +240,38 @@
             top = part if top is None else jnp.maximum(top, part)
         tops[side] = top
 
+    def weight_stage(c):
+        side = c % 2
+        top = jnp.max(tops[side], axis=0, keepdims=True)
+        total = None
+        for block in blocks:
+            part = jnp.exp2(scores[side, block] - top)
+            probs[c, block] = part.astype(BF16)
+            part = jnp.sum(part.reshape(CHIP // 8, 8, PAIR), axis=0)
+            total = part if total is None else total + part
+        inverse = 1.0 / jnp.sum(total, axis=0, keepdims=True)
+        inverse = jnp.broadcast_to(inverse, (CHIP, PAIR)).astype(BF16)
+        for block in blocks:
+            probs[c, block] = probs[c, block] * inverse
+
+    def sum_stage(c, part):
+        h = c // CHUNKS
+        left, right = ((changes, qb), (probs, gb))[part]
+        right = jnp.concatenate([right[h, :, col] for col in cols_of(c)], axis=0)
+        total = jnp.dot(left[c], right, preferred_element_type=F32)
+        if c % CHUNKS == 0:
+            acc[h, part] = total
+        else:
+            acc[h, part] += total
+
     def out_stage(c):
         h, side = c // CHUNKS, c % 2
-        top = jnp.max(tops[side], axis=0, keepdims=True)
-        for block in blocks:
-            weights[side, block] = jnp.exp2(scores[side, block] - top).astype(BF16)
-        out = jnp.dot(value_t[h % 2], weights[side], preferred_element_type=F32)
-        inverse = 1.0 / out[DH:DH + 1]
-        out = out[:DH] * inverse
+        out = jnp.dot(value_t[h % 2], probs[c], preferred_element_type=F32)
         cols = cols_of(c)
         grad = jnp.concatenate([gb[h, :, col].T for col in cols], axis=1)
         grad_t[side] = grad
         delta = jnp.sum(out.astype(BF16).astype(F32) * grad.astype(F32), axis=0, keepdims=True)
-        rows[side, 0] = jnp.broadcast_to(inverse, (8, PAIR))
-        rows[side, 1] = jnp.broadcast_to(delta, (8, PAIR))
+        rows[side] = jnp.broadcast_to(delta, (8, PAIR))
         out = out.T.astype(BF16)
         for i, col in enumerate(cols):
             ob[h, :, col] = out[i * CHIP:(i + 1) * CHIP]
@@ -271,70 +279,81 @@
     def change_stage(c):
         h, side = c // CHUNKS, c % 2
         raw = jnp.dot(kv[h, :, 1].reshape(KEYS, DH), grad_t[side], preferred_element_type=F32)
-        inverse = jnp.broadcast_to(rows[side, 0, 0:1], (CHIP, PAIR)).astype(BF16)
-        delta = rows[side, 1, 0:1]
+        delta = rows[side, 0:1]
         for block in blocks:
-            prob = weights[side, block] * inverse
-            probs[side, block] = prob
-            changes[c, block] = prob * (raw[block] - delta).astype(BF16)
-
-    def key_stage(c):
-        h = c // CHUNKS
-        for part, (left, right) in enumerate(((changes.at[c], qb), (probs.at[c % 2], gb))):
-            right = jnp.concatenate([right[h, :, col] for col in cols_of(c)], axis=0)
-            total = jnp.dot(left[...], right, preferred_element_type=F32)
-            if c % CHUNKS == 0:
-                acc[h, part] = total
-            else:
-                acc[h, part] += total
+            changes[c, block] = probs[c, block] * (raw[block] - delta).astype(BF16)
 
     def query_stage(h):
+        keys_t = kv[h, :, 0].reshape(KEYS, DH).T
         for c in range(h * CHUNKS, (h + 1) * CHUNKS):
-            query_grad = (jnp.dot(key_t[h], changes[c], preferred_element_type=F32) * SCALE).T.astype(BF16)
+            query_grad = (jnp.dot(keys_t, changes[c], preferred_element_type=F32) * SCALE).T.astype(BF16)
             for i, col in enumerate(cols_of(c)):
                 dqb[h, :, col] = query_grad[i * CHIP:(i + 1) * CHIP]
         give_out(h, 1)
 
-    after = {
-        1: [(pass_on, 2, 2), (pass_on, 3, 3)],
-        5: [(pass_on, 2, 1), (pass_on, 3, 2)],
-        9: [(pass_on, 3, 1)],
-        10: [(next_sum, 0, 1)],
-        14: [(next_sum, 0, 2), (next_sum, 1, 1)],
-    }
-    steps = HEADS * CHUNKS
-    for step in range(steps + 3):
-        if step < steps and step % CHUNKS == 0:
-            h = step // CHUNKS
+    def begin(h, part):
+        if part == 0:
             wait_rows(h)
-            for slot in (4, 0):
-                for part in range(2):
-                    wait_kv(h, slot, part)
-            prepare(h)
-        if step < steps:
-            score_stage(step)
-        if 0 <= step - 2 < steps:
-            change_stage(step - 2)
-        if 0 <= step - 1 < steps:
-            out_stage(step - 1)
-        if 0 <= step - 3:
-            key_stage(step - 3)
-            if (step - 3) % CHUNKS == CHUNKS - 1:
-                h = (step - 3) // CHUNKS
-                first_sum(h)
-                give_out(h, 0)
-        for event, *where in after.get(step, []):
-            event(*where)
-    for h, slot in ((0, 3), (1, 2), (2, 1)):
-        next_sum(h, slot)
-    query_stage(0)
-    query_stage(1)
-    for h, slot in ((0, 4), (1, 3), (2, 2), (3, 1)):
-        next_sum(h, slot)
-    query_stage(2)
-    query_stage(3)
-    for h, slot in ((1, 4), (2, 3), (3, 2), (2, 4), (3, 3), (3, 4)):
-        next_sum(h, slot)
+        for slot in (4, 0):
+            wait_kv(h, slot, part)
+        if part == 1:
+            value_t[h % 2] = kv[h, :, 1].reshape(KEYS, DH).T
+
+    def finish(h, part):
+        first_sum(h, 1 - part)
+        if part == 1:
+            give_out(h, 0)
+
+    def run(phases, after):
+        items = [(h, part, h * CHUNKS + p) for h, part in phases for p in range(CHUNKS)]
+        for step in range(len(items) + 2):
+            if step < len(items):
+                h, part, c = items[step]
+                if c % CHUNKS == 0:
+                    begin(h, part)
+                (score_stage, out_stage)[part](c)
+            if 0 <= step - 1 < len(items):
+                h, part, c = items[step - 1]
+                (weight_stage, change_stage)[part](c)
+            if 0 <= step - 2:
+                h, part, c = items[step - 2]
+                sum_stage(c, 1 - part)
+                if c % CHUNKS == CHUNKS - 1:
+                    finish(h, part)
+            for event, *where in after.get(step, []):
+                event(*where)
+
+    key, value = 0, 1
+    run(((0, 0), (0, 1), (1, 0), (1, 1)), {
+        3: [(pass_on, 2, 2, (key,)), (pass_on, 3, 3, (key,)), (pass_on, 2, 2, (value,)), (pass_on, 3, 3, (value,))],
+        11: [(pass_on, 2, 1, (key,)), (pass_on, 3, 2, (key,)), (pass_on, 2, 1, (value,)), (pass_on, 3, 2, (value,))],
+        14: [(next_sum, 0, value, 1)],
+        17: [(next_sum, 0, key, 1)],
+    })
+    pass_on(3, 1)
+    next_sum(1, value, 1)
+    next_sum(0, value, 2)
+    next_sum(1, key, 1)
+    run(((2, 0), (3, 0), (2, 1), (3, 1)), {
+        0: [(next_sum, 0, key, 2)],
+        4: [(next_sum, 1, value, 2)],
+        5: [(next_sum, 0, value, 3)],
+        8: [(next_sum, 1, key, 2)],
+        9: [(next_sum, 0, key, 3)],
+        13: [(next_sum, 1, value, 3)],
+        14: [(next_sum, 0, value, 4)],
+        15: [(next_sum, 2, value, 1)],
+        17: [(next_sum, 1, key, 3)],
+    })
+    for event, *where in (
+        (next_sum, 0, key, 4), (next_sum, 3, value, 1), (query_stage, 0), (next_sum, 1, value, 4),
+        (next_sum, 2, key, 1), (next_sum, 2, value, 2), (query_stage, 1), (next_sum, 1, key, 4),
+        (next_sum, 3, key, 1), (next_sum, 3, value, 2), (query_stage, 2), (next_sum, 2, key, 2),
+        (next_sum, 2, value, 3), (query_stage, 3), (next_sum, 3, key, 2), (next_sum, 3, value, 3),
+        (next_sum, 2, key, 3), (next_sum, 2, value, 4), (next_sum, 3, key, 3), (next_sum, 3, value, 4),
+        (next_sum, 2, key, 4), (next_sum, 3, key, 4),
+    ):
+        event(*where)
 
     for h in range(HEADS):
         for copy in own_to_ahead(h) + own_to_sibling(h) + rows_to_sibling(h):
@@ -394,14 +413,12 @@
                 pltpu.VMEM((HEADS, 2, CHIP, DH), BF16),
                 pltpu.VMEM((KEYS, DH), F32),
                 pltpu.VMEM((1, 128), jnp.int32),
-                pltpu.VMEM((HEADS, DH, KEYS), BF16),
-                pltpu.VMEM((2, DH + 16, KEYS), BF16),
+                pltpu.VMEM((2, DH, KEYS), BF16),
                 pltpu.VMEM((2, DH, PAIR), BF16),
                 pltpu.VMEM((2, KEYS, PAIR), F32),
                 pltpu.VMEM((2, 8, PAIR), F32),
-                pltpu.VMEM((2, 2, 8, PAIR), F32),
-                pltpu.VMEM((2, KEYS, PAIR), BF16),
-                pltpu.VMEM((2, KEYS, PAIR), BF16),
+                pltpu.VMEM((2, 8, PAIR), F32),
+                pltpu.VMEM((HEADS * CHUNKS, KEYS, PAIR), BF16),
                 pltpu.VMEM((HEADS * CHUNKS, KEYS, PAIR), BF16),
                 pltpu.VMEM((ROWS, 2 * HEADS * DH), BF16),
                 pltpu.VMEM((ROWS, 2 * HEADS * DH), BF16),

time: 74.4 us -> 69 us (0.927)
  Pallas kernels: 73.6 us -> 68.2 us
    pallas_call x1, Pallas kernels: 72.1 us -> 66.8 us  [per_device(): pl.pallas_call(functools.partial(kernel, devices), out_shape=tuple((pltpu...]
where the time goes in v6:
time: 69 us; the launch traced here: 68.9 us
  Pallas kernels  68.2 us (99%)
    pallas_call x1, Pallas kernels, per_device(): pl.pallas_call(functools.partial(kernel, devices), out_shape=tuple((pltpu...  66.8 us
    pallas_call x1, Pallas kernels, per_device(): pl.pallas_call(copy_out, out_shape=(wide, wide, narrow, narrow), in_specs...  1.48 us

profile of v6, /device:TPU:1, one launch (start us, length us, event | category | flops | bytes accessed | tf_op | source)
XLA Modules:
  0.0 68.9 jit_solution(18079523756778710806)
XLA Ops:
  0.6 66.8 %shard_map.84 = (bf16[64,8192]{1,0:T(8,128)(2,1)S(1)}, bf16[64,8192]{1,0:T(8,128)(2,1)S(1)}, bf16[64,1024]{1,0:T(8,128)(2,1)S(1)}, bf16[64,1024]{1,0:T(8,128)(2,1)S(1)}) custom-call(bf16[64,8192]{1,0:T(8,128)(2,1)} %q_in.1, bf16[64,1024]{1,0:T(8,128)(2,1)} %k_in.1, bf16[64,1024]{1,0:T(8,128)(2,1)} %v_in.1, bf16[64,8192]{1,0:T(8,128)(2,1)} %g_in.1, ...), custom_call_target="tpu_custom_call" | custom-call | flops 4026531840 | bytes 5242880 | tf_op jit(solution)/shard_map/pallas_call | solution.py:399
  67.4 1.5 %shard_map.85 = (bf16[64,8192]{1,0:T(8,128)(2,1)}, bf16[64,8192]{1,0:T(8,128)(2,1)}, bf16[64,1024]{1,0:T(8,128)(2,1)}, bf16[64,1024]{1,0:T(8,128)(2,1)}) custom-call(bf16[64,8192]{1,0:T(8,128)(2,1)S(1)} %get-tuple-element.8.refs_0_, bf16[64,8192]{1,0:T(8,128)(2,1)S(1)} %get-tuple-element.9.refs_1_, bf16[64,1024]{1,0:T(8,128)(2,1)S(1)} %get-tuple-element.10.refs_2_, ...), custom_call_target="tpu_custom_call" | custom-call | tf_op jit(solution)/shard_map/pallas_call | solution.py:452

commit v7 on v6

--- a/solution.py
+++ b/solution.py
@@ -64,8 +64,8 @@
 
     def own_to_ahead(h):
         made = []
-        for side, (owner, target) in enumerate(((core, ahead), (other, ahead_other))):
-            for part, src in enumerate((k_own, v_own)):
+        for part, src in enumerate((k_own, v_own)):
+            for side, (owner, target) in enumerate(((core, ahead), (other, ahead_other))):
                 made.append(remote(
                     src.at[:, head_cols(owner, h, DH)], kv.at[h, 3, part, my_rows],
                     own_ici.at[h, side, part], kv_recv.at[h, 3, part], target,
@@ -325,8 +325,8 @@
 
     key, value = 0, 1
     run(((0, 0), (0, 1), (1, 0), (1, 1)), {
-        3: [(pass_on, 2, 2, (key,)), (pass_on, 3, 3, (key,)), (pass_on, 2, 2, (value,)), (pass_on, 3, 3, (value,))],
-        11: [(pass_on, 2, 1, (key,)), (pass_on, 3, 2, (key,)), (pass_on, 2, 1, (value,)), (pass_on, 3, 2, (value,))],
+        5: [(pass_on, 2, 2, (key,)), (pass_on, 3, 3, (key,)), (pass_on, 2, 2, (value,)), (pass_on, 3, 3, (value,))],
+        13: [(pass_on, 2, 1, (key,)), (pass_on, 3, 2, (key,)), (pass_on, 2, 1, (value,)), (pass_on, 3, 2, (value,))],
         14: [(next_sum, 0, value, 1)],
         17: [(next_sum, 0, key, 1)],
     })
@@ -335,15 +335,14 @@
     next_sum(0, value, 2)
     next_sum(1, key, 1)
     run(((2, 0), (3, 0), (2, 1), (3, 1)), {
-        0: [(next_sum, 0, key, 2)],
-        4: [(next_sum, 1, value, 2)],
-        5: [(next_sum, 0, value, 3)],
-        8: [(next_sum, 1, key, 2)],
-        9: [(next_sum, 0, key, 3)],
-        13: [(next_sum, 1, value, 3)],
-        14: [(next_sum, 0, value, 4)],
-        15: [(next_sum, 2, value, 1)],
-        17: [(next_sum, 1, key, 3)],
+        2: [(next_sum, 0, key, 2)],
+        6: [(next_sum, 1, value, 2)],
+        7: [(next_sum, 0, value, 3)],
+        10: [(next_sum, 1, key, 2)],
+        11: [(next_sum, 0, key, 3)],
+        15: [(next_sum, 1, value, 3)],
+        16: [(next_sum, 0, value, 4)],
+        17: [(next_sum, 2, value, 1), (next_sum, 1, key, 3)],
     })
     for event, *where in (
         (next_sum, 0, key, 4), (next_sum, 3, value, 1), (query_stage, 0), (next_sum, 1, value, 4),

time: 69 us -> 68.4 us (level)
  no operation moved by 1% of the time
where the time goes in v7:
time: 68.4 us; the launch traced here: 68.2 us
  Pallas kernels  67.6 us (99%)
    pallas_call x1, Pallas kernels, per_device(): pl.pallas_call(functools.partial(kernel, devices), out_shape=tuple((pltpu...  66.1 us
    pallas_call x1, Pallas kernels, per_device(): pl.pallas_call(copy_out, out_shape=(wide, wide, narrow, narrow), in_specs...  1.48 us

profile of v7, /device:TPU:1, one launch (start us, length us, event | category | flops | bytes accessed | tf_op | source)
XLA Modules:
  0.0 68.2 jit_solution(5763494001433817916)
XLA Ops:
  0.6 66.1 %shard_map.84 = (bf16[64,8192]{1,0:T(8,128)(2,1)S(1)}, bf16[64,8192]{1,0:T(8,128)(2,1)S(1)}, bf16[64,1024]{1,0:T(8,128)(2,1)S(1)}, bf16[64,1024]{1,0:T(8,128)(2,1)S(1)}) custom-call(bf16[64,8192]{1,0:T(8,128)(2,1)} %q_in.1, bf16[64,1024]{1,0:T(8,128)(2,1)} %k_in.1, bf16[64,1024]{1,0:T(8,128)(2,1)} %v_in.1, bf16[64,8192]{1,0:T(8,128)(2,1)} %g_in.1, ...), custom_call_target="tpu_custom_call" | custom-call | flops 4026531840 | bytes 5242880 | tf_op jit(solution)/shard_map/pallas_call | solution.py:398
  66.8 1.5 %shard_map.85 = (bf16[64,8192]{1,0:T(8,128)(2,1)}, bf16[64,8192]{1,0:T(8,128)(2,1)}, bf16[64,1024]{1,0:T(8,128)(2,1)}, bf16[64,1024]{1,0:T(8,128)(2,1)}) custom-call(bf16[64,8192]{1,0:T(8,128)(2,1)S(1)} %get-tuple-element.8.refs_0_, bf16[64,8192]{1,0:T(8,128)(2,1)S(1)} %get-tuple-element.9.refs_1_, bf16[64,1024]{1,0:T(8,128)(2,1)S(1)} %get-tuple-element.10.refs_2_, ...), custom_call_target="tpu_custom_call" | custom-call | tf_op jit(solution)/shard_map/pallas_call | solution.py:451

commit v8 on v7

--- a/solution.py
+++ b/solution.py
@@ -47,6 +47,8 @@
 
     sibling = (cp, hd + 1 - 2 * core)
     chip_base = me - core
+    chip = chip_base // 2
+    not_last = chip < devices // 2 - 1
     ahead = device(me + 2)
     ahead_other = device(chip_base + 2 + other)
     behind = device(me - 2)
@@ -114,6 +116,9 @@
             for part, (src, dst) in enumerate(((q_in, qb), (g_in, gb)))
         ]
 
+    def reaches(slot):
+        return chip >= 4 - slot
+
     def start(copies):
         for copy in copies:
             copy.start()
@@ -131,12 +136,19 @@
                       kv_fwd.at[h, slot - 1, part], kv_recv.at[h, slot - 1, part], ahead)
 
     def own_ahead(h):
-        start(own_to_ahead(h))
+        @pl.when(not_last)
+        def _():
+            start(own_to_ahead(h))
 
     def pass_on(h, slot, parts=(0, 1)):
         for part in parts:
-            wait_kv(h, slot, part)
-            forward(h, slot, part).start()
+            @pl.when(reaches(slot))
+            def _():
+                wait_kv(h, slot, part)
+
+            @pl.when(reaches(slot) & not_last)
+            def _():
+                forward(h, slot, part).start()
 
     def sum_copy(h, slot, part):
         return remote(gout.at[h, slot, part], gin.at[h, slot, part],
@@ -144,16 +156,25 @@
 
     def first_sum(h, part):
         gout[h, 0, part] = (acc[h, part, 0:CHIP] * (SCALE, 1.0)[part]).astype(BF16)
-        sum_copy(h, 0, part).start()
+        @pl.when(reaches(0))
+        def _():
+            sum_copy(h, 0, part).start()
 
     def next_sum(h, part, slot):
         ref = gin.at[h, slot - 1, part]
-        pltpu.make_async_copy(ref, ref, sum_recv.at[h, slot - 1, part]).wait()
+
+        @pl.when(reaches(slot) & not_last)
+        def _():
+            pltpu.make_async_copy(ref, ref, sum_recv.at[h, slot - 1, part]).wait()
+
         mine = acc[h, part, slot * CHIP:(slot + 1) * CHIP] * (SCALE, 1.0)[part]
         total = gin[h, slot - 1, part].astype(F32) + mine
         if slot < 4:
             gout[h, slot, part] = total.astype(BF16)
-            sum_copy(h, slot, part).start()
+
+            @pl.when(reaches(slot))
+            def _():
+                sum_copy(h, slot, part).start()
         else:
             fin[h, part] = total.astype(BF16)
             fin_remote(h, part).start()
@@ -174,9 +195,22 @@
         out_remote(h, part).start()
         (att_out, dq_out)[part][:, head_cols(core, h, WIDE)] = (ob, dqb)[part][h, my_rows]
 
+    for slot in range(4):
+        @pl.when(chip < 4 - slot)
+        def _():
+            kv[:, slot] = jnp.zeros((HEADS, 2, CHIP, DH), BF16)
+
+    @pl.when(chip == devices // 2 - 1)
+    def _():
+        gin[...] = jnp.zeros(gin.shape, BF16)
+
     barrier = pltpu.get_barrier_semaphore()
-    for peer in (sibling, ahead, ahead_other, behind, behind_other):
-        pl.semaphore_signal(barrier, inc=1, device_id=peer, device_id_type=MESH)
+    for joined, peers in ((chip >= 0, (sibling,)), (not_last, (ahead, ahead_other)), (chip > 0, (behind, behind_other))):
+        @pl.when(joined)
+        def _():
+            for peer in peers:
+                pl.semaphore_signal(barrier, inc=1, device_id=peer, device_id_type=MESH)
+
     len_copy = pltpu.make_async_copy(len_in, lens, len_sem)
     len_copy.start()
     start(stage_kv())
@@ -186,7 +220,7 @@
         start(rows_local(h))
     for copy in stage_kv():
         copy.wait()
-    pl.semaphore_wait(barrier, 5)
+    pl.semaphore_wait(barrier, 1 + 2 * (not_last.astype(jnp.int32) + (chip > 0).astype(jnp.int32)))
 
     for h in range(2):
         own_ahead(h)
@@ -294,8 +328,12 @@
     def begin(h, part):
         if part == 0:
             wait_rows(h)
-        for slot in (4, 0):
-            wait_kv(h, slot, part)
+        wait_kv(h, 4, part)
+
+        @pl.when(reaches(0))
+        def _():
+            wait_kv(h, 0, part)
+
         if part == 1:
             value_t[h % 2] = kv[h, :, 1].reshape(KEYS, DH).T
 
@@ -355,13 +393,27 @@
         event(*where)
 
     for h in range(HEADS):
-        for copy in own_to_ahead(h) + own_to_sibling(h) + rows_to_sibling(h):
+        for copy in own_to_sibling(h) + rows_to_sibling(h):
             copy.wait_send()
+
+        @pl.when(not_last)
+        def _():
+            for copy in own_to_ahead(h):
+                copy.wait_send()
+
+        for slot in range(4):
+            @pl.when(reaches(slot))
+            def _():
+                for part in range(2):
+                    sum_copy(h, slot, part).wait_send()
+
+        for slot in (3, 2, 1):
+            @pl.when(reaches(slot) & not_last)
+            def _():
+                for part in range(2):
+                    forward(h, slot, part).wait_send()
+
         for part in range(2):
-            for slot in (3, 2, 1):
-                forward(h, slot, part).wait_send()
-            for slot in range(4):
-                sum_copy(h, slot, part).wait_send()
             out_remote(h, part).wait_send()
             fin_remote(h, part).wait_send()
         for part, dst in enumerate((att_out, dq_out)):

time: 68.4 us -> 66.4 us (0.971)
  the two profiles are of different devices: /device:TPU:1 before, /device:TPU:7 now
where the time goes in v8:
time: 66.4 us; the launch traced here: 66.2 us
  Pallas kernels  65.6 us (99%)
    pallas_call x1, Pallas kernels, per_device(): pl.pallas_call(functools.partial(kernel, devices), out_shape=tuple((pltpu...  64.1 us
    pallas_call x1, Pallas kernels, per_device(): pl.pallas_call(copy_out, out_shape=(wide, wide, narrow, narrow), in_specs...  1.48 us

profile of v8, /device:TPU:7, one launch (start us, length us, event | category | flops | bytes accessed | tf_op | source)
XLA Modules:
  0.0 66.2 jit_solution(14642448312716997015)
XLA Ops:
  0.6 64.1 %shard_map.84 = (bf16[64,8192]{1,0:T(8,128)(2,1)S(1)}, bf16[64,8192]{1,0:T(8,128)(2,1)S(1)}, bf16[64,1024]{1,0:T(8,128)(2,1)S(1)}, bf16[64,1024]{1,0:T(8,128)(2,1)S(1)}) custom-call(bf16[64,8192]{1,0:T(8,128)(2,1)} %q_in.1, bf16[64,1024]{1,0:T(8,128)(2,1)} %k_in.1, bf16[64,1024]{1,0:T(8,128)(2,1)} %v_in.1, bf16[64,8192]{1,0:T(8,128)(2,1)} %g_in.1, ...), custom_call_target="tpu_custom_call" | custom-call | flops 4026531840 | bytes 5242880 | tf_op jit(solution)/shard_map/pallas_call | solution.py:450
  64.7 1.5 %shard_map.85 = (bf16[64,8192]{1,0:T(8,128)(2,1)}, bf16[64,8192]{1,0:T(8,128)(2,1)}, bf16[64,1024]{1,0:T(8,128)(2,1)}, bf16[64,1024]{1,0:T(8,128)(2,1)}) custom-call(bf16[64,8192]{1,0:T(8,128)(2,1)S(1)} %get-tuple-element.8.refs_0_, bf16[64,8192]{1,0:T(8,128)(2,1)S(1)} %get-tuple-element.9.refs_1_, bf16[64,1024]{1,0:T(8,128)(2,1)S(1)} %get-tuple-element.10.refs_2_, ...), custom_call_target="tpu_custom_call" | custom-call | tf_op jit(solution)/shard_map/pallas_call | solution.py:503
